TPU v7x, 256 devices: a whole 4x4x8 slice. The times are simulated.
256 devices in a mesh: nodes: 256 (over x, z, y, core).
Axes of the slice: x: 4, y: 4, z: 8, core: 2. Of those that a mesh axis runs over, the one named last changes fastest.
Arguments:
- features: bfloat16 [131072, 512], P('nodes'), may hold values from -6 to 6
- norm_gain: float32 [512], replicated, may hold values from 0.25 to 1.75
- w_query: bfloat16 [512, 512], replicated, may hold values from -0.25 to 0.25
- key_weight: bfloat16 [512, 512], replicated, may hold values from -0.25 to 0.25
- value_weight: bfloat16 [512, 512], replicated, may hold values from -0.25 to 0.25
- w_out: bfloat16 [512, 512], replicated, may hold values from -0.25 to 0.25
- virtual_states: bfloat16 [256, 128], P('nodes'), may hold values from -6 to 6
- block_pairs: int32 [4096, 2], P('nodes'), may hold values from 0 to 3, as said below
- block_masks: int32 [4096, 128, 128], P('nodes'), may hold values 0 or 1
- pair_counts: int32 [256], P('nodes'), may hold values from 2 to 16
- partners: int32 [256, 4, 4], P('nodes'), may hold values from 0 to 3, as said below
Outputs:
- attended: bfloat16 [131072, 512], P('nodes')
Inputs may be any that keep to these rules, and one draw needn't show every extreme that they name: `block_pairs`: within one device the 16 slots name distinct (query block, key block) pairs. `partners`: for each m and each device pair (d, d xor 2^bit_m) the two rows are inverse permutations of the 4 local blocks.
All inputs are finite; a program needn't handle non-finite values. No bound on the sum of `block_masks` on one device may be relied on, other than what follows from the above.
Results may differ from a plain program's by a relative error of at most 0.0084.
Values may be sent and summed in bfloat16 or wider, within the bound.
A program may use at most 64 MiB of HBM per device.

v0:
```python
import jax
import jax.numpy as jnp
from jax import lax
from jax.sharding import PartitionSpec as P

HEAD_COUNT = 8
VIRTUAL_NODES = 64


EPSILON = 1e-05


def partner(block, axis, bit):
    count = lax.axis_size(axis)
    route = []
    for low in range(count):
        high = low | 1 << bit
        if high != low and high < count:
            route += [(low, high), (high, low)]
    return lax.ppermute(block, axis, route)


def norm_rows(rows, norm_gain):
    floats = rows.astype(jnp.float32)
    center = floats - jnp.mean(floats, axis=-1, keepdims=True)
    variance = jnp.mean(center * center, axis=-1, keepdims=True)
    return (center * lax.rsqrt(variance + EPSILON) * norm_gain).astype(jnp.bfloat16)


def apply_projection(rows, weight):
    return jnp.dot(rows, weight, preferred_element_type=jnp.float32).astype(jnp.bfloat16)


def attend(state, queries, keys_in, values_in, score_scale, keep):
    numerator, denominator = state
    scores = (
        jnp.einsum("bhqd,bhkd->bhqk", queries, keys_in, preferred_element_type=jnp.float32)
        * score_scale
    )
    weights = jnp.exp(scores) * keep
    denominator = denominator + jnp.sum(weights, axis=-1)
    numerator = numerator + jnp.einsum(
        "bhqk,bhkd->bhqd",
        weights.astype(jnp.bfloat16),
        values_in,
        preferred_element_type=jnp.float32,
    )
    return (numerator, denominator)


def local(
    features,
    norm_gain,
    w_query,
    key_weight,
    value_weight,
    w_out,
    virtual_states,
    block_pairs,
    block_masks,
    pair_counts,
    partners,
):
    node_rows = features.shape[0]
    model_width = features.shape[1]
    head_width = model_width // HEAD_COUNT
    block_size = block_masks.shape[1]
    total_blocks = node_rows // block_size
    score_scale = float(head_width) ** (-0.5)

    def split_heads(rows):
        return rows.reshape(total_blocks, block_size, HEAD_COUNT, head_width).transpose(0, 2, 1, 3)

    normed = norm_rows(features, norm_gain)
    q_heads = split_heads(apply_projection(normed, w_query))
    own_keys = apply_projection(normed, key_weight)
    own_vals = apply_projection(normed, value_weight)
    k_heads = split_heads(own_keys)
    v_heads = split_heads(own_vals)
    gathered = lax.all_gather(virtual_states, "nodes", axis=0, tiled=True)
    virtual_norm = norm_rows(gathered.reshape(VIRTUAL_NODES, model_width), norm_gain)
    virtual_keys = (
        apply_projection(virtual_norm, key_weight)
        .reshape(VIRTUAL_NODES, HEAD_COUNT, head_width)
        .transpose(1, 0, 2)
    )
    virtual_values = (
        apply_projection(virtual_norm, value_weight)
        .reshape(VIRTUAL_NODES, HEAD_COUNT, head_width)
        .transpose(1, 0, 2)
    )
    numerator = jnp.zeros((total_blocks, HEAD_COUNT, block_size, head_width), jnp.float32)
    denominator = jnp.zeros((total_blocks, HEAD_COUNT, block_size), jnp.float32)
    live_count = pair_counts[0]
    group_total = block_pairs.shape[0] // 4

    def slot_group(group_idx, state):
        start = group_idx * 4
        pair_rows = lax.dynamic_slice_in_dim(block_pairs, start, 4, 0)
        mask_rows = lax.dynamic_slice_in_dim(block_masks, start, 4, 0)
        valid = (start + jnp.arange(4, dtype=jnp.int32) < live_count).astype(jnp.float32)
        keep = mask_rows[:, None].astype(jnp.float32) * valid[:, None, None, None]
        empty = (
            jnp.zeros((4, HEAD_COUNT, block_size, head_width), jnp.float32),
            jnp.zeros((4, HEAD_COUNT, block_size), jnp.float32),
        )
        part_num, part_den = attend(
            empty,
            jnp.take(q_heads, pair_rows[:, 0], axis=0),
            jnp.take(k_heads, pair_rows[:, 1], axis=0),
            jnp.take(v_heads, pair_rows[:, 1], axis=0),
            score_scale,
            keep,
        )
        total_num, total_den = state
        for slot in range(4):
            target = pair_rows[slot, 0]
            held_num = lax.dynamic_slice_in_dim(total_num, target, 1, 0)
            total_num = lax.dynamic_update_slice_in_dim(
                total_num, held_num + part_num[slot : slot + 1], target, 0
            )
            held_den = lax.dynamic_slice_in_dim(total_den, target, 1, 0)
            total_den = lax.dynamic_update_slice_in_dim(
                total_den, held_den + part_den[slot : slot + 1], target, 0
            )
        return (total_num, total_den)

    numerator, denominator = lax.fori_loop(0, group_total, slot_group, (numerator, denominator))
    logn = lax.axis_size("nodes").bit_length() - 1
    match_bits = (0, 1, logn - 2, logn - 1)
    for matching in range(4):
        got_keys, got_vals = partner((own_keys, own_vals), "nodes", match_bits[matching])
        partner_idx = partners[0, matching]
        far_keys = jnp.take(split_heads(got_keys), partner_idx, axis=0)
        far_vals = jnp.take(split_heads(got_vals), partner_idx, axis=0)
        numerator, denominator = attend(
            (numerator, denominator), q_heads, far_keys, far_vals, score_scale, 1.0
        )
    broadened_keys = jnp.broadcast_to(
        virtual_keys[None], (total_blocks, HEAD_COUNT, VIRTUAL_NODES, head_width)
    )
    broadened_values = jnp.broadcast_to(
        virtual_values[None], (total_blocks, HEAD_COUNT, VIRTUAL_NODES, head_width)
    )
    numerator, denominator = attend(
        (numerator, denominator), q_heads, broadened_keys, broadened_values, score_scale, 1.0
    )
    mixed = (
        (numerator / denominator[..., None])
        .transpose(0, 2, 1, 3)
        .reshape(node_rows, model_width)
        .astype(jnp.bfloat16)
    )
    return jnp.dot(mixed, w_out, preferred_element_type=jnp.float32).astype(jnp.bfloat16)


def solution(mesh):
    placed = (
        P("nodes", None),
        P(),
        P(),
        P(),
        P(),
        P(),
        P("nodes", None),
        P("nodes", None),
        P("nodes", None, None),
        P("nodes"),
        P("nodes", None, None),
    )
    return jax.shard_map(
        local, mesh=mesh, in_specs=placed, out_specs=P("nodes", None), check_vma=False
    )
```

profile of v0, /device:TPU:1, one launch (start us, length us, event | category | flops | bytes accessed | tf_op | source)
XLA Modules:
  0.0 273.2 jit_solution(16904593629791803729)
XLA Ops:
  2.7 2.3 convolution_convert_fusion.2
  5.0 3.2 %collective-permute-start = (bf16[512,512]{1,0:T(8,128)(2,1)}, bf16[512,512]{1,0:T(8,128)(2,1)}, u32[]{:S(2)}, u32[]{:S(2)}) collective-permute-start(bf16[512,512]{1,0:T(8,128)(2,1)} %convolution_convert_fusion.2), channel_id=1, source_target_pairs={{0,1},{1,0},{2,3},{3,2},{4,5},{5,4},{6,7},{7,6},{8,9},{9,8},{10,11... | collective-permute-start | bytes 1572872 | tf_op jit(solution)/shard_map/ppermute | solution.py:20
  12.7 2.1 copy.76
  14.8 71.0 %all-gather = bf16[256,1,128]{2,1,0:T(2,128)(2,1)S(1)} all-gather(bf16[1,1,128]{2,1,0:T(2,128)(2,1)S(1)} %bitcast.88), channel_id=1, replica_groups=mesh['nodes'=256] {'nodes'}, dimensions={0}, use_global_device_ids=true | all-gather | bytes 65792 | tf_op jit(solution)/shard_map/all_gather | solution.py:80
  93.0 117.5 %while.15 = (s32[]{:T(128)}, f32[4,8,128,64]{2,3,1,0:T(8,128)}, f32[4,8,128]{2,1,0:T(8,128)S(1)}, s32[16,2]{0,1:T(2,128)S(1)}, bf16[4,8,128,64]{3,2,1,0:T(8,128)...) while((s32[]{:T(128)}, f32[4,8,128,64]{2,3,1,0:T(8,128)}, ...), condition=%wide.region_4.6_spmd, body=%wide.region_2.5_spmd.sunk | while | flops 138545216 | bytes 23667424 | solution.py:128
  100.8 3.8 %fusion.125 = (f32[4,8,128]{2,1,0:T(8,128)S(1)}, f32[4,8,128,128]{2,3,1,0:T(8,128)}) fusion(f32[4,128,128]{1,2,0:T(8,128)S(1)} %convert_multiply_fusion.2, bf16[4,8,128,64]{3,2,1,0:T(8,128)(2,1)} %gather_fusion, pred[4]{0:T(512)(128)(4,1)S(1)} %get-tuple-element.325, bf16[4,8,128,64]{3,2,1,0:T(8,128)(2,1)} %gather_fusion.1, ...), kind=kOutput, calls=%fused_computation.12.clone.1 | convolution fusion | flops 69201920 | bytes 3424264 | tf_op jit(solution)/shard_map/while/body/eval_jaxpr/bhqd,bhkd->bhqk/dot_general | solution.py:37
  104.6 2.0 gather_fusion.2
  106.6 2.3 fusion.126
  130.2 3.8 %fusion.125 = (f32[4,8,128]{2,1,0:T(8,128)S(1)}, f32[4,8,128,128]{2,3,1,0:T(8,128)}) fusion(f32[4,128,128]{1,2,0:T(8,128)S(1)} %convert_multiply_fusion.2, bf16[4,8,128,64]{3,2,1,0:T(8,128)(2,1)} %gather_fusion, pred[4]{0:T(512)(128)(4,1)S(1)} %get-tuple-element.325, bf16[4,8,128,64]{3,2,1,0:T(8,128)(2,1)} %gather_fusion.1, ...), kind=kOutput, calls=%fused_computation.12.clone.1 | convolution fusion | flops 69201920 | bytes 3424264 | tf_op jit(solution)/shard_map/while/body/eval_jaxpr/bhqd,bhkd->bhqk/dot_general | solution.py:37
  134.0 2.0 gather_fusion.2
  136.0 2.3 fusion.126
  159.6 3.8 %fusion.125 = (f32[4,8,128]{2,1,0:T(8,128)S(1)}, f32[4,8,128,128]{2,3,1,0:T(8,128)}) fusion(f32[4,128,128]{1,2,0:T(8,128)S(1)} %convert_multiply_fusion.2, bf16[4,8,128,64]{3,2,1,0:T(8,128)(2,1)} %gather_fusion, pred[4]{0:T(512)(128)(4,1)S(1)} %get-tuple-element.325, bf16[4,8,128,64]{3,2,1,0:T(8,128)(2,1)} %gather_fusion.1, ...), kind=kOutput, calls=%fused_computation.12.clone.1 | convolution fusion | flops 69201920 | bytes 3424264 | tf_op jit(solution)/shard_map/while/body/eval_jaxpr/bhqd,bhkd->bhqk/dot_general | solution.py:37
  163.4 2.0 gather_fusion.2
  165.4 2.3 fusion.126
  189.0 3.8 %fusion.125 = (f32[4,8,128]{2,1,0:T(8,128)S(1)}, f32[4,8,128,128]{2,3,1,0:T(8,128)}) fusion(f32[4,128,128]{1,2,0:T(8,128)S(1)} %convert_multiply_fusion.2, bf16[4,8,128,64]{3,2,1,0:T(8,128)(2,1)} %gather_fusion, pred[4]{0:T(512)(128)(4,1)S(1)} %get-tuple-element.325, bf16[4,8,128,64]{3,2,1,0:T(8,128)(2,1)} %gather_fusion.1, ...), kind=kOutput, calls=%fused_computation.12.clone.1 | convolution fusion | flops 69201920 | bytes 3424264 | tf_op jit(solution)/shard_map/while/body/eval_jaxpr/bhqd,bhkd->bhqk/dot_general | solution.py:37
  194.8 2.3 fusion.126
  219.0 2.4 reshape.232
  223.1 2.4 reshape.233
  229.3 2.4 reshape.234
  233.4 2.4 reshape.235
  240.3 2.4 reshape.236
  244.4 2.4 reshape.237
  251.4 2.4 reshape.238
  255.5 2.4 reshape.239
  (214 shorter events, 116.2 us)
Async XLA Ops:
  0.0 2.7 copy-start
  0.0 8.3 %copy-start.12 = (bf16[512,512]{1,0:T(8,128)(2,1)S(1)}, bf16[512,512]{1,0:T(8,128)(2,1)}, u32[]{:S(2)}) copy-start(bf16[512,512]{1,0:T(8,128)(2,1)} %param.15) | copy-start | bytes 1572868
  0.0 8.3 %copy-start.16 = (f32[512]{0:T(512)S(1)}, f32[512]{0:T(512)}, u32[]{:S(2)}) copy-start(f32[512]{0:T(512)} %param.16) | copy-start | bytes 6148
  0.0 8.3 %copy-start.13 = (bf16[512,512]{1,0:T(8,128)(2,1)S(1)}, bf16[512,512]{1,0:T(8,128)(2,1)}, u32[]{:S(2)}) copy-start(bf16[512,512]{1,0:T(8,128)(2,1)} %param.19) | copy-start | bytes 1572868
  5.0 9.7 %copy-start.18 = (bf16[1,128]{1,0:T(2,128)(2,1)S(1)}, bf16[1,128]{1,0:T(2,128)(2,1)}, u32[]{:S(2)}) copy-start(bf16[1,128]{1,0:T(2,128)(2,1)} %param.21) | copy-start | bytes 772
  5.0 81.9 %copy-start.19 = (bf16[512,512]{1,0:T(8,128)(2,1)S(1)}, bf16[512,512]{1,0:T(8,128)(2,1)}, u32[]{:S(2)}) copy-start(bf16[512,512]{1,0:T(8,128)(2,1)} %param.17) | copy-start | bytes 1572868
  5.0 207.9 %collective-permute-start = (bf16[512,512]{1,0:T(8,128)(2,1)}, bf16[512,512]{1,0:T(8,128)(2,1)}, u32[]{:S(2)}, u32[]{:S(2)}) collective-permute-start(bf16[512,512]{1,0:T(8,128)(2,1)} %convolution_convert_fusion.2), channel_id=1, source_target_pairs={{0,1},{1,0},{2,3},{3,2},{4,5},{5,4},{6,7},{7,6},{8,9},{9,8},{10,11... | collective-permute-start | bytes 1572872 | tf_op jit(solution)/shard_map/ppermute | solution.py:20
  8.3 207.2 %collective-permute-start.2 = (bf16[512,512]{1,0:T(8,128)(2,1)}, bf16[512,512]{1,0:T(8,128)(2,1)}, u32[]{:S(2)}, u32[]{:S(2)}) collective-permute-start(bf16[512,512]{1,0:T(8,128)(2,1)} %convolution_convert_fusion.2), channel_id=1, source_target_pairs={{0,2},{2,0},{1,3},{3,1},{4,6},{6,4},{5,7},{7,5},{8,10},{10,8},{9,1... | collective-permute-start | bytes 1572872 | tf_op jit(solution)/shard_map/ppermute | solution.py:20
  9.6 204.3 %collective-permute-start.1 = (bf16[512,512]{1,0:T(8,128)(2,1)}, bf16[512,512]{1,0:T(8,128)(2,1)}, u32[]{:S(2)}, u32[]{:S(2)}) collective-permute-start(bf16[512,512]{1,0:T(8,128)(2,1)} %convolution_convert_fusion.1), channel_id=1, source_target_pairs={{0,1},{1,0},{2,3},{3,2},{4,5},{5,4},{6,7},{7,6},{8,9},{9,8},{10,11... | collective-permute-start | bytes 1572872 | tf_op jit(solution)/shard_map/ppermute | solution.py:20
  9.7 223.7 %collective-permute-start.3 = (bf16[512,512]{1,0:T(8,128)(2,1)}, bf16[512,512]{1,0:T(8,128)(2,1)}, u32[]{:S(2)}, u32[]{:S(2)}) collective-permute-start(bf16[512,512]{1,0:T(8,128)(2,1)} %convolution_convert_fusion.1), channel_id=1, source_target_pairs={{0,2},{2,0},{1,3},{3,1},{4,6},{6,4},{5,7},{7,5},{8,10},{10,8},{9,1... | collective-permute-start | bytes 1572872 | tf_op jit(solution)/shard_map/ppermute | solution.py:20
  11.4 228.9 %collective-permute-start.4 = (bf16[512,512]{1,0:T(8,128)(2,1)}, bf16[512,512]{1,0:T(8,128)(2,1)}, u32[]{:S(2)}, u32[]{:S(2)}) collective-permute-start(bf16[512,512]{1,0:T(8,128)(2,1)} %convolution_convert_fusion.2), channel_id=1, source_target_pairs={{0,64},{64,0},{1,65},{65,1},{2,66},{66,2},{3,67},{67,3},{4,68},{68... | collective-permute-start | bytes 1572872 | tf_op jit(solution)/shard_map/ppermute | solution.py:20
  89.3 3.7 %copy-start.15 = (s32[16,2]{0,1:T(2,128)S(1)}, s32[16,2]{0,1:T(2,128)}, u32[]{:S(2)}) copy-start(s32[16,2]{0,1:T(2,128)} %param.22) | copy-start | bytes 388
  93.0 123.9 %copy-start.17 = (s32[1,4,4]{2,1,0:T(4,128)S(1)}, s32[1,4,4]{2,1,0:T(4,128)}, u32[]{:S(2)}) copy-start(s32[1,4,4]{2,1,0:T(4,128)} %param.25) | copy-start | bytes 196
  93.0 7.8 %copy-start.3 = (bf16[4,8,128,64]{3,2,1,0:T(8,128)(2,1)}, bf16[4,8,128,64]{3,2,1,0:T(8,128)(2,1)S(1)}, u32[]{:S(2)}) copy-start(bf16[4,8,128,64]{3,2,1,0:T(8,128)(2,1)S(1)} %get-tuple-element.364) | copy-start | bytes 1572868 | tf_op jit(solution)/shard_map/while
  109.8 12.4 %copy-start.4 = (bf16[4,8,128,64]{3,2,1,0:T(8,128)(2,1)S(1)}, bf16[4,8,128,64]{3,2,1,0:T(8,128)(2,1)}, u32[]{:S(2)}) copy-start(bf16[4,8,128,64]{3,2,1,0:T(8,128)(2,1)} %copy-done.3) | copy-start | bytes 1572868 | tf_op jit(solution)/shard_map/while
  122.2 8.0 %copy-start.3 = (bf16[4,8,128,64]{3,2,1,0:T(8,128)(2,1)}, bf16[4,8,128,64]{3,2,1,0:T(8,128)(2,1)S(1)}, u32[]{:S(2)}) copy-start(bf16[4,8,128,64]{3,2,1,0:T(8,128)(2,1)S(1)} %get-tuple-element.364) | copy-start | bytes 1572868 | tf_op jit(solution)/shard_map/while
  139.2 12.4 %copy-start.4 = (bf16[4,8,128,64]{3,2,1,0:T(8,128)(2,1)S(1)}, bf16[4,8,128,64]{3,2,1,0:T(8,128)(2,1)}, u32[]{:S(2)}) copy-start(bf16[4,8,128,64]{3,2,1,0:T(8,128)(2,1)} %copy-done.3) | copy-start | bytes 1572868 | tf_op jit(solution)/shard_map/while
  151.7 8.0 %copy-start.3 = (bf16[4,8,128,64]{3,2,1,0:T(8,128)(2,1)}, bf16[4,8,128,64]{3,2,1,0:T(8,128)(2,1)S(1)}, u32[]{:S(2)}) copy-start(bf16[4,8,128,64]{3,2,1,0:T(8,128)(2,1)S(1)} %get-tuple-element.364) | copy-start | bytes 1572868 | tf_op jit(solution)/shard_map/while
  168.7 12.4 %copy-start.4 = (bf16[4,8,128,64]{3,2,1,0:T(8,128)(2,1)S(1)}, bf16[4,8,128,64]{3,2,1,0:T(8,128)(2,1)}, u32[]{:S(2)}) copy-start(bf16[4,8,128,64]{3,2,1,0:T(8,128)(2,1)} %copy-done.3) | copy-start | bytes 1572868 | tf_op jit(solution)/shard_map/while
  181.1 8.0 %copy-start.3 = (bf16[4,8,128,64]{3,2,1,0:T(8,128)(2,1)}, bf16[4,8,128,64]{3,2,1,0:T(8,128)(2,1)S(1)}, u32[]{:S(2)}) copy-start(bf16[4,8,128,64]{3,2,1,0:T(8,128)(2,1)S(1)} %get-tuple-element.364) | copy-start | bytes 1572868 | tf_op jit(solution)/shard_map/while
  198.1 12.4 %copy-start.4 = (bf16[4,8,128,64]{3,2,1,0:T(8,128)(2,1)S(1)}, bf16[4,8,128,64]{3,2,1,0:T(8,128)(2,1)}, u32[]{:S(2)}) copy-start(bf16[4,8,128,64]{3,2,1,0:T(8,128)(2,1)} %copy-done.3) | copy-start | bytes 1572868 | tf_op jit(solution)/shard_map/while
  212.9 31.5 %collective-permute-start.5 = (bf16[512,512]{1,0:T(8,128)(2,1)}, bf16[512,512]{1,0:T(8,128)(2,1)}, u32[]{:S(2)}, u32[]{:S(2)}) collective-permute-start(bf16[512,512]{1,0:T(8,128)(2,1)} %convolution_convert_fusion.1), channel_id=1, source_target_pairs={{0,64},{64,0},{1,65},{65,1},{2,66},{66,2},{3,67},{67,3},{4,68},{68... | collective-permute-start | bytes 1572872 | tf_op jit(solution)/shard_map/ppermute | solution.py:20
  213.9 37.5 %collective-permute-start.6 = (bf16[512,512]{1,0:T(8,128)(2,1)}, bf16[512,512]{1,0:T(8,128)(2,1)}, u32[]{:S(2)}, u32[]{:S(2)}) collective-permute-start(bf16[512,512]{1,0:T(8,128)(2,1)} %convolution_convert_fusion.2), channel_id=1, source_target_pairs={{0,128},{128,0},{1,129},{129,1},{2,130},{130,2},{3,131},{131,3},{4... | collective-permute-start | bytes 1572872 | tf_op jit(solution)/shard_map/ppermute | solution.py:20
  215.4 40.1 %collective-permute-start.7 = (bf16[512,512]{1,0:T(8,128)(2,1)}, bf16[512,512]{1,0:T(8,128)(2,1)}, u32[]{:S(2)}, u32[]{:S(2)}) collective-permute-start(bf16[512,512]{1,0:T(8,128)(2,1)} %convolution_convert_fusion.1), channel_id=1, source_target_pairs={{0,128},{128,0},{1,129},{129,1},{2,130},{130,2},{3,131},{131,3},{4... | collective-permute-start | bytes 1572872 | tf_op jit(solution)/shard_map/ppermute | solution.py:20
  (14 other events, 14.9 us)
where the time goes:
time: 276 us; the launch traced here: 273 us
  local copies, waits for them, and re-layouts  89 us (32%)
  blocking collectives  71 us (26%)
  matrix products  39.1 us (14%)
  other arithmetic  35.9 us (13%)
  loops' own time  28.8 us (10%)
  starting transfers between devices  8.98 us (3%)
    all_gather x1, blocking collectives, local(): gathered = lax.all_gather(virtual_states, 'nodes', axis=0, tiled=True)  71 us
    reshape x19, local copies, waits for them, and re-layouts, split_heads(): rows.reshape(total_blocks, block_size, HEAD_COUNT, head_width)  34.3 us
    another operation x1, loops' own time, local(): lax.fori_loop(0, group_total, slot_group, (numerator, denominator))  28.8 us
    dynamic_update_slice x16, other arithmetic, slot_group(): lax.dynamic_update_slice_in_dim(total_num, held_num + part_num[slot:slot...  28.5 us
    dot_general x9, matrix products, attend(): jnp.einsum('bhqd,bhkd->bhqk', queries, keys_in, preferred_element_type=jn...  20.7 us
    dot_general x9, matrix products, attend(): jnp.einsum('bhqk,bhkd->bhqd', weights.astype(jnp.bfloat16), values_in, pr...  11.4 us
    ppermute x8, starting transfers between devices, partner(): return lax.ppermute(block, axis, route)  8.98 us
    gather x4, local copies, waits for them, and re-layouts, slot_group(): jnp.take(v_heads, pair_rows[:, 1], axis=0)  7.88 us
  transfers between devices with their start and end apart: 8, of which 0 were waited for; matrix products, arithmetic and copies ran while one was open for 50% of the time, Pallas kernels for 0%

commit v1 on v0

v1 whole, which is shorter than its diff:
```python
import functools

import jax
import jax.numpy as jnp
from jax import lax
from jax.experimental import pallas as pl
from jax.experimental.pallas import tpu as pltpu
from jax.sharding import PartitionSpec as P

HEADS = 8
WIDTH = 512
HEAD = 64
BLK = 128
BLOCKS = 4
ROWS = BLK * BLOCKS
SLOTS = 16
VIRTUAL = 64
PAIR = 4
EPSILON = 1e-05
SCORE_SCALE = 1.4426950408889634 / 8.0
RELAY = 64
RELAYS = ROWS // RELAY
PER_BLOCK = BLK // RELAY
MESH = pl.DeviceIdType.MESH
BF = jnp.bfloat16
F32 = jnp.float32


def norm_rows(floats, gain):
    center = floats - jnp.mean(floats, axis=-1, keepdims=True)
    variance = jnp.mean(center * center, axis=-1, keepdims=True)
    return (center * lax.rsqrt(variance + EPSILON) * gain).astype(BF)


def scores(q, k2):
    return lax.dot_general(q, k2, (((1,), (1,)), ((), ())), preferred_element_type=F32)


def dot(a, b):
    return jnp.dot(a, b, preferred_element_type=F32)


def lane_halves(rows):
    lane = lax.broadcasted_iota(jnp.int32, (rows, BLK), 1)
    even = jnp.where(lane < HEAD, 1.0, 0.0).astype(BF)
    odd = jnp.where(lane < HEAD, 0.0, 1.0).astype(BF)
    return even, odd


def kernel(
    features, gain_ref, w_query, key_weight, value_weight, w_out, virtual_row, pairs, masks, counts, partners,
    out_ref,
    raw, normed, wq, wkv, wo, mask_raw, keep, qs, own_k, own_v, land_core, core_k, core_v, land, far_k, far_v,
    virt_k, virt_v, gather, near, far_acc,
    local_sem, send_row, recv_row, send_core, recv_core, send_y, recv_y, send_x, recv_x, send_relay, recv_relay,
):
    me = lax.axis_index("nodes")
    core = me % 2
    y = (me // 2) % 4
    z = (me // 8) % 8
    x = me // 64
    y_near = y + 1 - 2 * (y % 2)
    x_near = x + 1 - 2 * (x % 2)

    def device(xx, zz, yy, cc):
        return xx * 64 + zz * 8 + yy * 2 + cc

    core_peer = device(x, z, y, 1 - core)
    y_peer = device(x, z, y_near, core)
    x_peer = device(x_near, z, y, core)
    relay_peer = device(3 - x, z, y, core)
    first = []
    for dx in range(4):
        for flip_y in range(2):
            for flip_core in range(2):
                if dx or flip_y or flip_core:
                    first.append(
                        device((x + dx) % 4, z, y_near if flip_y else y, 1 - core if flip_core else core)
                    )
    second = device(x, z, 3 - y, core)
    third = [device(x, (z + dz) % 8, y, core) for dz in range(1, 8)]
    peers = first + [second] + third

    barrier = pltpu.get_barrier_semaphore()
    for peer in peers:
        pl.semaphore_signal(barrier, inc=1, device_id=(peer,), device_id_type=MESH)

    def fetch(src, dst, index):
        copy = pltpu.make_async_copy(src, dst, local_sem.at[index])
        copy.start()
        return copy

    get_features = fetch(features, raw, 0)
    get_query = fetch(w_query, wq, 1)
    get_key = fetch(key_weight, wkv.at[:, pl.ds(0, WIDTH)], 2)
    get_value = fetch(value_weight, wkv.at[:, pl.ds(WIDTH, WIDTH)], 3)
    get_masks = fetch(masks, mask_raw, 4)
    get_out = fetch(w_out, wo, 5)

    gain = gain_ref[...]
    yc = y * 2 + core
    gather[x, z, pl.ds(yc, 1)] = virtual_row[...].astype(F32)
    get_features.wait()
    for block in range(BLOCKS):
        rows = pl.ds(block * BLK, BLK)
        normed[rows] = norm_rows(raw[rows].astype(F32), gain)

    def remote(src, dst, send, recv, peer):
        return pltpu.make_async_remote_copy(
            src_ref=src, dst_ref=dst, send_sem=send, recv_sem=recv, device_id=(peer,), device_id_type=MESH
        )

    def x_copy(r):
        c, part = r // PER_BLOCK, r % PER_BLOCK
        return remote(
            normed.at[pl.ds(r * RELAY, RELAY)],
            land.at[c, 1, pl.ds(part * RELAY, RELAY)],
            send_x.at[r], recv_x.at[r], x_peer,
        )

    def relay_copy(r):
        c, part = r // PER_BLOCK, r % PER_BLOCK
        return remote(
            land.at[c, 1, pl.ds(part * RELAY, RELAY)],
            land.at[c + 1, 2, pl.ds(part * RELAY, RELAY)],
            send_relay.at[r], recv_relay.at[r], relay_peer,
        )

    def y_copy(c):
        return remote(normed.at[pl.ds(c * BLK, BLK)], land.at[c, 0], send_y.at[c], recv_y.at[c], y_peer)

    copy_core = remote(normed, land_core, send_core.at[0], recv_core.at[0], core_peer)
    mine = gather.at[x, z, pl.ds(yc, 1)]
    copy_first = [remote(mine, mine, send_row.at[i], recv_row.at[i], peer) for i, peer in enumerate(first)]
    four = gather.at[:, z, pl.ds(4 * (y // 2), 4)]
    copy_second = remote(four, four, send_row.at[15], recv_row.at[15], second)
    plane = gather.at[:, z]
    copy_third = [remote(plane, plane, send_row.at[16 + i], recv_row.at[16 + i], peer) for i, peer in enumerate(third)]

    pl.semaphore_wait(barrier, len(peers))
    for copy in copy_first:
        copy.start()
    for c in range(BLOCKS):
        for part in range(PER_BLOCK):
            x_copy(c * PER_BLOCK + part).start()
        y_copy(c).start()
    copy_core.start()

    def relay(r):
        x_copy(r).wait_recv()
        relay_copy(r).start()

    even, odd = lane_halves(BLK)
    get_query.wait()
    for j in range(PAIR):
        part = dot(normed[...], wq[:, j * BLK:(j + 1) * BLK]) * SCORE_SCALE
        for b in range(BLOCKS):
            qs[b, j] = part[b * BLK:(b + 1) * BLK].astype(BF)

    def project(rows, place_k, place_v, blocks):
        for j in range(PAIR):
            part = dot(rows, wkv[:, j * BLK:(j + 1) * BLK])
            for b in range(blocks):
                piece = part[b * BLK:(b + 1) * BLK].astype(BF)
                ref = place_k(b, j)
                ref[0:BLK] = piece * even
                ref[BLK:2 * BLK] = piece * odd
            part = dot(rows, wkv[:, WIDTH + j * BLK:WIDTH + (j + 1) * BLK])
            for b in range(blocks):
                piece = part[b * BLK:(b + 1) * BLK].astype(BF)
                ref = place_v(b, j)
                ref[0:BLK] = piece * even
                ref[BLK:2 * BLK] = piece * odd

    get_key.wait()
    get_value.wait()
    project(normed[...], lambda b, j: own_k.at[j, b], lambda b, j: own_v.at[j, b], BLOCKS)

    ones = jnp.concatenate([even, odd], axis=0)

    def widen(v2):
        return jnp.concatenate([v2, ones], axis=1)

    get_masks.wait()
    live = counts[0]
    for qb in range(BLOCKS):
        for kb in range(BLOCKS):
            slot = jnp.int32(0)
            for s in range(SLOTS):
                slot = jnp.where((pairs[s, 0] == qb) & (pairs[s, 1] == kb), s, slot)
            alive = jnp.where(slot < live, 1, 0)
            keep[qb, kb] = (mask_raw[slot] * alive).astype(F32).astype(BF)

    for copy in copy_first:
        copy.wait_recv()
    copy_second.start()

    @pl.loop(0, PAIR)
    def _(j):
        for b in range(BLOCKS):
            q = qs[b, j]
            total = None
            for kb in range(BLOCKS):
                p = jnp.exp2(scores(q, own_k[j, kb])).astype(BF)
                mask = keep[b, kb]
                p = p * jnp.concatenate([mask, mask], axis=1)
                part = dot(p, widen(own_v[j, kb]))
                total = part if total is None else total + part
            near[b, j] = total

    copy_second.wait_recv()
    for copy in copy_third:
        copy.start()
    relay(0)

    copy_core.wait_recv()
    project(land_core[...], lambda b, j: core_k.at[b, j], lambda b, j: core_v.at[b, j], BLOCKS)
    relay(1)

    @pl.loop(0, PAIR)
    def _(j):
        for b in range(BLOCKS):
            key_block = partners[0, b]
            p = jnp.exp2(scores(qs[b, j], core_k[key_block, j])).astype(BF)
            near[b, j] += dot(p, widen(core_v[key_block, j]))

    def far_step(c, sources):
        lo, hi = sources[0], sources[-1] + 1
        rows = land[c, lo:hi].reshape((hi - lo) * BLK, WIDTH)
        project(rows, lambda b, j: far_k.at[lo + b, j], lambda b, j: far_v.at[lo + b, j], hi - lo)
        for m in sources:
            block = c - 1 if m == 2 else c
            target = jnp.int32(0)
            for b in range(BLOCKS):
                target = jnp.where(partners[m + 1, b] == block, b, target)
            for j in range(PAIR):
                p = jnp.exp2(scores(qs[target, j], far_k[m, j])).astype(BF)
                far_acc[m, block, j] = dot(p, widen(far_v[m, j]))

    def arrive(c):
        for part in range(PER_BLOCK):
            r = c * PER_BLOCK + part
            if not isinstance(c, int) or r > 1:
                relay(r)
        y_copy(c).wait_recv()

    def arrive_relayed(c):
        for part in range(PER_BLOCK):
            relay_copy(c * PER_BLOCK + part).wait_recv()

    arrive(0)
    far_step(0, (0, 1))

    @pl.loop(1, BLOCKS)
    def _(c):
        arrive(c)
        arrive_relayed(c - 1)
        far_step(c, (0, 1, 2))

    for copy in copy_third:
        copy.wait_recv()
    even_v, odd_v = lane_halves(VIRTUAL)
    ones_v = jnp.concatenate([even_v, odd_v], axis=0)
    table = gather.reshape(256, BLK)
    state = jnp.concatenate([table[pl.ds(i, VIRTUAL, stride=4), :] for i in range(4)], axis=1)
    virtual_norm = norm_rows(state, gain)
    virtual_kv = dot(virtual_norm, wkv[...]).astype(BF)
    for j in range(PAIR):
        piece = virtual_kv[:, j * BLK:(j + 1) * BLK]
        virt_k[j, 0:VIRTUAL] = piece * even_v
        virt_k[j, VIRTUAL:2 * VIRTUAL] = piece * odd_v
        piece = virtual_kv[:, WIDTH + j * BLK:WIDTH + (j + 1) * BLK]
        virt_v[j, 0:VIRTUAL] = piece * even_v
        virt_v[j, VIRTUAL:2 * VIRTUAL] = piece * odd_v

    @pl.loop(0, PAIR)
    def _(j):
        wide = jnp.concatenate([virt_v[j], ones_v], axis=1)
        for b in range(BLOCKS):
            p = jnp.exp2(scores(qs[b, j], virt_k[j])).astype(BF)
            near[b, j] += (
                dot(p, wide) + far_acc[0, partners[1, b], j] + far_acc[1, partners[2, b], j]
            )

    get_out.wait()
    arrive_relayed(BLOCKS - 1)
    far_step(BLOCKS, (2,))

    for b in range(BLOCKS):
        mixed = []
        for j in range(PAIR):
            total = near[b, j] + far_acc[2, partners[3, b], j]
            mixed.append((total[:, 0:BLK] / total[:, BLK:2 * BLK]).astype(BF))
        out_ref[b * BLK:(b + 1) * BLK] = dot(jnp.concatenate(mixed, axis=1), wo[...]).astype(BF)

    for copy in copy_first + [copy_second] + copy_third + [copy_core]:
        copy.wait_send()
    for r in range(RELAYS):
        x_copy(r).wait_send()
        relay_copy(r).wait_send()
    for c in range(BLOCKS):
        y_copy(c).wait_send()


def local(
    features, norm_gain, w_query, key_weight, value_weight, w_out, virtual_states, block_pairs, block_masks,
    pair_counts, partners,
):
    anywhere = pl.BlockSpec(memory_space=pl.ANY)
    vmem = pl.BlockSpec(memory_space=pltpu.VMEM)
    smem = pl.BlockSpec(memory_space=pltpu.SMEM)
    dma = pltpu.SemaphoreType.DMA
    return pl.pallas_call(
        kernel,
        out_shape=jax.ShapeDtypeStruct((ROWS, WIDTH), BF),
        in_specs=[anywhere, vmem, anywhere, anywhere, anywhere, anywhere, vmem, smem, anywhere, smem, smem],
        out_specs=vmem,
        scratch_shapes=[
            pltpu.VMEM((ROWS, WIDTH), BF),
            pltpu.VMEM((ROWS, WIDTH), BF),
            pltpu.VMEM((WIDTH, WIDTH), BF),
            pltpu.VMEM((WIDTH, 2 * WIDTH), BF),
            pltpu.VMEM((WIDTH, WIDTH), BF),
            pltpu.VMEM((SLOTS, BLK, BLK), jnp.int32),
            pltpu.VMEM((BLOCKS, BLOCKS, BLK, BLK), BF),
            pltpu.VMEM((BLOCKS, PAIR, BLK, BLK), BF),
            pltpu.VMEM((PAIR, BLOCKS, 2 * BLK, BLK), BF),
            pltpu.VMEM((PAIR, BLOCKS, 2 * BLK, BLK), BF),
            pltpu.VMEM((ROWS, WIDTH), BF),
            pltpu.VMEM((BLOCKS, PAIR, 2 * BLK, BLK), BF),
            pltpu.VMEM((BLOCKS, PAIR, 2 * BLK, BLK), BF),
            pltpu.VMEM((BLOCKS + 1, 3, BLK, WIDTH), BF),
            pltpu.VMEM((3, PAIR, 2 * BLK, BLK), BF),
            pltpu.VMEM((3, PAIR, 2 * BLK, BLK), BF),
            pltpu.VMEM((PAIR, BLK, BLK), BF),
            pltpu.VMEM((PAIR, BLK, BLK), BF),
            pltpu.VMEM((4, 8, 8, BLK), F32),
            pltpu.VMEM((BLOCKS, PAIR, BLK, 2 * BLK), F32),
            pltpu.VMEM((3, BLOCKS, PAIR, BLK, 2 * BLK), F32),
            dma((6,)),
            dma((23,)), dma((23,)),
            dma((1,)), dma((1,)),
            dma((BLOCKS,)), dma((BLOCKS,)),
            dma((RELAYS,)), dma((RELAYS,)),
            dma((RELAYS,)), dma((RELAYS,)),
        ],
        compiler_params=pltpu.CompilerParams(
            collective_id=0, has_side_effects=True, vmem_limit_bytes=48 * 1024 * 1024
        ),
        cost_estimate=pl.CostEstimate(flops=8_000_000_000, bytes_accessed=4_500_000, transcendentals=4_500_000),
        name="expander_layer",
    )(
        features, norm_gain.reshape(1, WIDTH), w_query, key_weight, value_weight, w_out, virtual_states,
        block_pairs, block_masks, pair_counts, partners.reshape(4, BLOCKS),
    )


def solution(mesh):
    placed = (
        P("nodes", None), P(), P(), P(), P(), P(), P("nodes", None), P("nodes", None), P("nodes", None, None),
        P("nodes"), P("nodes", None, None),
    )
    return jax.shard_map(local, mesh=mesh, in_specs=placed, out_specs=P("nodes", None), check_vma=False)
```

time: 276 us -> 45.8 us (0.17)
  local copies, waits for them, and re-layouts: 89 us -> 8.59 us
  blocking collectives: 71 us -> 0 us
  matrix products: 39.1 us -> 0 us
  Pallas kernels: 0 us -> 36.2 us
  other arithmetic: 35.9 us -> 0 us
  loops' own time: 28.8 us -> 0 us
  starting transfers between devices: 8.98 us -> 0 us
    all_gather x1 -> x0, blocking collectives: 71 us -> none  [local(): gathered = lax.all_gather(virtual_states, 'nodes', axis=0, tiled=True)]
    dot_general x24 -> x0, matrix products: 39.1 us -> none  [the longest x9 20.7 us: attend(): jnp.einsum('bhqd,bhkd->bhqk', queries, keys_in, preferred_element_type=jn...]
    pallas_call x0 -> x1, Pallas kernels: none -> 36.2 us  [local(): pl.pallas_call(kernel, out_shape=jax.ShapeDtypeStruct((ROWS, WIDTH), BF),...]
    reshape x21 -> x0, local copies, waits for them, and re-layouts: 34.5 us -> none  [the longest x19 34.3 us: split_heads(): rows.reshape(total_blocks, block_size, HEAD_COUNT, head_width)]
    gather x20 -> x0, local copies, waits for them, and re-layouts: 31.9 us -> none  [the longest x4 7.88 us: slot_group(): jnp.take(v_heads, pair_rows[:, 1], axis=0)]
    another operation x1 -> x0, loops' own time: 28.8 us -> none  [local(): lax.fori_loop(0, group_total, slot_group, (numerator, denominator))]
    dynamic_update_slice x32 -> x0, other arithmetic: 28.6 us -> none  [the longest x16 28.5 us: slot_group(): lax.dynamic_update_slice_in_dim(total_num, held_num + part_num[slot:slot...]
    ppermute x8 -> x0, starting transfers between devices: 8.98 us -> none  [partner(): return lax.ppermute(block, axis, route)]
  transfers between devices with their start and end apart: 8 -> 0, of which waited for: 0 -> 0; matrix products, arithmetic and copies ran while one was open for 50% -> 0% of each run, Pallas kernels for 0% -> 0%
where the time goes in v1:
time: 45.8 us; the launch traced here: 45.4 us
  Pallas kernels  36.2 us (79%)
  local copies, waits for them, and re-layouts  8.59 us (19%)
  between operations  0.68 us (1%)
    pallas_call x1, Pallas kernels, local(): pl.pallas_call(kernel, out_shape=jax.ShapeDtypeStruct((ROWS, WIDTH), BF),...  36.2 us
    unnamed x22, local copies, waits for them, and re-layouts  8.59 us

profile of v1, /device:TPU:1, one launch (start us, length us, event | category | flops | bytes accessed | tf_op | source)
XLA Modules:
  0.0 45.4 jit_solution(9138616769049741843)
XLA Ops:
  0.7 0.0 copy-start.9
  0.7 0.7 %copy-done.9 = s32[16,2]{0,1:T(2,128)S(1)} copy-done((s32[16,2]{0,1:T(2,128)S(1)}, s32[16,2]{0,1:T(2,128)}, u32[]{:S(2)}) %copy-start.9) | copy-done | bytes 152
  1.3 0.0 copy-start.6
  1.3 0.0 copy-start.7
  1.3 0.0 copy-start.8
  1.3 0.1 copy.12.pairs
  1.4 0.6 %copy-done.6 = f32[512]{0:T(512)S(1)} copy-done((f32[512]{0:T(512)S(1)}, f32[512]{0:T(512)}, u32[]{:S(2)}) %copy-start.6) | copy-done | bytes 2072
  2.0 0.0 copy-done.7
  2.0 0.0 copy-done.8
  2.0 0.0 copy-start
  2.0 1.2 %copy-done = s32[16,128,128]{2,1,0:T(8,128)S(1)} copy-done((s32[16,128,128]{2,1,0:T(8,128)S(1)}, s32[16,128,128]{2,1,0:T(8,128)}, u32[]{:S(2)}) %copy-start) | copy-done | bytes 1048600
  3.3 0.0 copy-start.1
  3.3 1.0 %copy-done.1 = bf16[512,512]{1,0:T(8,128)(2,1)S(1)} copy-done((bf16[512,512]{1,0:T(8,128)(2,1)S(1)}, bf16[512,512]{1,0:T(8,128)(2,1)}, u32[]{:S(2)}) %copy-start.1) | copy-done | bytes 524312
  4.3 0.0 copy-start.2
  4.3 1.0 %copy-done.2 = bf16[512,512]{1,0:T(8,128)(2,1)S(1)} copy-done((bf16[512,512]{1,0:T(8,128)(2,1)S(1)}, bf16[512,512]{1,0:T(8,128)(2,1)}, u32[]{:S(2)}) %copy-start.2) | copy-done | bytes 524312
  5.3 0.0 copy-start.3
  5.3 1.0 %copy-done.3 = bf16[512,512]{1,0:T(8,128)(2,1)S(1)} copy-done((bf16[512,512]{1,0:T(8,128)(2,1)S(1)}, bf16[512,512]{1,0:T(8,128)(2,1)}, u32[]{:S(2)}) %copy-start.3) | copy-done | bytes 524312
  6.4 0.0 copy-start.4
  6.4 1.0 %copy-done.4 = bf16[512,512]{1,0:T(8,128)(2,1)S(1)} copy-done((bf16[512,512]{1,0:T(8,128)(2,1)S(1)}, bf16[512,512]{1,0:T(8,128)(2,1)}, u32[]{:S(2)}) %copy-start.4) | copy-done | bytes 524312
  7.4 0.0 copy-start.5
  7.4 1.0 %copy-done.5 = bf16[512,512]{1,0:T(8,128)(2,1)S(1)} copy-done((bf16[512,512]{1,0:T(8,128)(2,1)S(1)}, bf16[512,512]{1,0:T(8,128)(2,1)}, u32[]{:S(2)}) %copy-start.5) | copy-done | bytes 524312
  8.5 36.2 %expander_layer.1 = bf16[512,512]{1,0:T(8,128)(2,1)S(1)} custom-call(bf16[512,512]{1,0:T(8,128)(2,1)S(1)} %copy-done.1, f32[1,512]{1,0:T(1,128)S(1)} %bitcast.2, bf16[512,512]{1,0:T(8,128)(2,1)S(1)} %copy-done.2, bf16[512,512]{1,0:T(8,128)(2,1)S(1)} %copy-done.3, bf16[512,512]{1,0:T(8,128)(2,1)S(1)} %copy-done.4, bf16[512,512]{1,0:T(8,128)(2,1)S(1)} %copy-done.5, ...), custom_call_target="tpu_custom_call" | custom-call | flops 8000000000 | bytes 4500000 | tf_op jit(solution)/shard_map/expander_layer/pallas_call | solution.py:313
  44.6 0.8 %copy.15 = bf16[512,512]{1,0:T(8,128)(2,1)} copy(bf16[512,512]{1,0:T(8,128)(2,1)S(1)} %expander_layer.1) | data formatting | bytes 1048576
Async XLA Ops:
  0.7 0.7 %copy-start.9 = (s32[16,2]{0,1:T(2,128)S(1)}, s32[16,2]{0,1:T(2,128)}, u32[]{:S(2)}) copy-start(s32[16,2]{0,1:T(2,128)} %param.18) | copy-start | bytes 388
  1.3 0.7 %copy-start.6 = (f32[512]{0:T(512)S(1)}, f32[512]{0:T(512)}, u32[]{:S(2)}) copy-start(f32[512]{0:T(512)} %param.12) | copy-start | bytes 6148
  1.3 0.7 %copy-start.7 = (s32[1,4,4]{2,1,0:T(4,128)S(1)}, s32[1,4,4]{2,1,0:T(4,128)}, u32[]{:S(2)}) copy-start(s32[1,4,4]{2,1,0:T(4,128)} %param.21) | copy-start | bytes 196
  1.3 0.7 %copy-start.8 = (bf16[1,128]{1,0:T(2,128)(2,1)S(1)}, bf16[1,128]{1,0:T(2,128)(2,1)}, u32[]{:S(2)}) copy-start(bf16[1,128]{1,0:T(2,128)(2,1)} %virtual_row.1) | copy-start | bytes 772
  2.0 1.2 %copy-start = (s32[16,128,128]{2,1,0:T(8,128)S(1)}, s32[16,128,128]{2,1,0:T(8,128)}, u32[]{:S(2)}) copy-start(s32[16,128,128]{2,1,0:T(8,128)} %masks.1) | copy-start | bytes 3145732
  3.3 1.0 %copy-start.1 = (bf16[512,512]{1,0:T(8,128)(2,1)S(1)}, bf16[512,512]{1,0:T(8,128)(2,1)}, u32[]{:S(2)}) copy-start(bf16[512,512]{1,0:T(8,128)(2,1)} %features.1) | copy-start | bytes 1572868
  4.3 1.0 %copy-start.2 = (bf16[512,512]{1,0:T(8,128)(2,1)S(1)}, bf16[512,512]{1,0:T(8,128)(2,1)}, u32[]{:S(2)}) copy-start(bf16[512,512]{1,0:T(8,128)(2,1)} %w_query.1) | copy-start | bytes 1572868
  5.3 1.0 %copy-start.3 = (bf16[512,512]{1,0:T(8,128)(2,1)S(1)}, bf16[512,512]{1,0:T(8,128)(2,1)}, u32[]{:S(2)}) copy-start(bf16[512,512]{1,0:T(8,128)(2,1)} %key_weight.1) | copy-start | bytes 1572868
  6.4 1.0 %copy-start.4 = (bf16[512,512]{1,0:T(8,128)(2,1)S(1)}, bf16[512,512]{1,0:T(8,128)(2,1)}, u32[]{:S(2)}) copy-start(bf16[512,512]{1,0:T(8,128)(2,1)} %value_weight.1) | copy-start | bytes 1572868
  7.4 1.0 %copy-start.5 = (bf16[512,512]{1,0:T(8,128)(2,1)S(1)}, bf16[512,512]{1,0:T(8,128)(2,1)}, u32[]{:S(2)}) copy-start(bf16[512,512]{1,0:T(8,128)(2,1)} %w_out.1) | copy-start | bytes 1572868

commit v2 on v1

v2 whole, which is shorter than its diff:
```python
import jax
import jax.numpy as jnp
from jax import lax
from jax.experimental import pallas as pl
from jax.experimental.pallas import tpu as pltpu
from jax.sharding import PartitionSpec as P

WIDTH = 512
HEAD = 64
BLK = 128
BLOCKS = 4
ROWS = BLK * BLOCKS
SLOTS = 16
VIRTUAL = 64
PAIR = 4
EPSILON = 1e-05
SCORE_SCALE = 1.4426950408889634 / 8.0
RELAY = 64
RELAYS = ROWS // RELAY
PER_BLOCK = BLK // RELAY
MESH = pl.DeviceIdType.MESH
BF = jnp.bfloat16
F32 = jnp.float32


def norm_rows(floats, gain):
    center = floats - jnp.mean(floats, axis=-1, keepdims=True)
    variance = jnp.mean(center * center, axis=-1, keepdims=True)
    return (center * lax.rsqrt(variance + EPSILON) * gain).astype(BF)


def scores(q, k2):
    return lax.dot_general(q, k2, (((1,), (1,)), ((), ())), preferred_element_type=F32)


def dot(a, b):
    return jnp.dot(a, b, preferred_element_type=F32)


def lane_halves(rows):
    lane = lax.broadcasted_iota(jnp.int32, (rows, BLK), 1)
    even = jnp.where(lane < HEAD, 1.0, 0.0).astype(BF)
    odd = jnp.where(lane < HEAD, 0.0, 1.0).astype(BF)
    return even, odd


def kernel(
    features, norm_gain, w_query, key_weight, value_weight, virtual_states, block_pairs, masks, counts, partner_blocks,
    out_ref,
    gain_ref, virtual_row, pairs, partners, raw, normed, wq, wkv, mask_raw, keep, qs, own_k, own_v, land_core, core_k,
    core_v, land, far_k, far_v, virt_k, virt_v, gather, near, far_acc, weights, far_w,
    local_sem, send_row, recv_row, send_core, recv_core, send_y, recv_y, send_x, recv_x, send_relay, recv_relay,
):
    me = lax.axis_index("nodes")
    core = me % 2
    y = (me // 2) % 4
    z = (me // 8) % 8
    x = me // 64
    y_near = y + 1 - 2 * (y % 2)
    x_near = x + 1 - 2 * (x % 2)

    def device(xx, zz, yy, cc):
        return xx * 64 + zz * 8 + yy * 2 + cc

    core_peer = device(x, z, y, 1 - core)
    y_peer = device(x, z, y_near, core)
    x_peer = device(x_near, z, y, core)
    relay_peer = device(3 - x, z, y, core)
    plane = []
    for dx in range(4):
        for flip_y in range(2):
            for flip_core in range(2):
                if dx or flip_y or flip_core:
                    plane.append(
                        device((x + dx) % 4, z, y_near if flip_y else y, 1 - core if flip_core else core)
                    )
    half = y // 2
    rank = jnp.where(z < 4, z * 2 + half, 8 + half * 4 + z - 4)

    def ranked(r):
        zz = jnp.where(r < 8, r // 2, 4 + r % 4)
        hh = jnp.where(r < 8, r % 2, (r - 8) // 4)
        return device(x, zz, jnp.where(hh == half, y, 3 - y), core)

    steps = range(1, 16)
    columns = {k: ranked((rank + k) % 16) for k in steps}

    def higher(k):
        return rank + k < 16

    barrier = pltpu.get_barrier_semaphore()
    for peer in plane:
        pl.semaphore_signal(barrier, inc=1, device_id=(peer,), device_id_type=MESH)
    for k in steps:
        @pl.when(higher(k))
        def _(k=k):
            pl.semaphore_signal(barrier, inc=1, device_id=(columns[k],), device_id_type=MESH)

    def fetch(src, dst, index):
        copy = pltpu.make_async_copy(src, dst, local_sem.at[index])
        copy.start()
        return copy

    get_features = fetch(features, raw, 0)
    get_gain = fetch(norm_gain, gain_ref, 1)
    get_row = fetch(virtual_states, virtual_row, 2)
    get_query = fetch(w_query, wq, 3)
    get_key = fetch(key_weight, wkv.at[:, pl.ds(0, WIDTH)], 4)
    get_value = fetch(value_weight, wkv.at[:, pl.ds(WIDTH, WIDTH)], 5)
    get_pairs = fetch(block_pairs, pairs, 6)
    get_partners = fetch(partner_blocks, partners, 7)
    get_masks = fetch(masks, mask_raw, 8)

    group = z * 2 + y // 2
    member = x * 4 + (y % 2) * 2 + core
    get_row.wait()
    gather[group, pl.ds(member, 1)] = virtual_row[...].astype(F32)
    get_gain.wait()
    gain = gain_ref[...]
    get_features.wait()
    for block in range(BLOCKS):
        rows = pl.ds(block * BLK, BLK)
        normed[rows] = norm_rows(raw[rows].astype(F32), gain)

    def remote(src, dst, send, recv, peer):
        return pltpu.make_async_remote_copy(
            src_ref=src, dst_ref=dst, send_sem=send, recv_sem=recv, device_id=(peer,), device_id_type=MESH
        )

    def x_copy(r):
        c, part = r // PER_BLOCK, r % PER_BLOCK
        return remote(
            normed.at[pl.ds(r * RELAY, RELAY)],
            land.at[c, 1, pl.ds(part * RELAY, RELAY)],
            send_x.at[r], recv_x.at[r], x_peer,
        )

    def relay_copy(r):
        c, part = r // PER_BLOCK, r % PER_BLOCK
        return remote(
            land.at[c, 1, pl.ds(part * RELAY, RELAY)],
            land.at[c + 1, 2, pl.ds(part * RELAY, RELAY)],
            send_relay.at[r], recv_relay.at[r], relay_peer,
        )

    def y_copy(c):
        return remote(normed.at[pl.ds(c * BLK, BLK)], land.at[c, 0], send_y.at[c], recv_y.at[c], y_peer)

    copy_core = remote(normed, land_core, send_core.at[0], recv_core.at[0], core_peer)
    mine = gather.at[group, pl.ds(member, 1)]
    copy_plane = [remote(mine, mine, send_row.at[i], recv_row.at[i], peer) for i, peer in enumerate(plane)]
    sixteen = gather.at[group]

    def column_copy(k):
        return remote(sixteen, sixteen, send_row.at[14 + k], recv_row.at[14 + k], columns[k])

    def column_arrived(k):
        column_copy(16 - k).wait_recv()

    def send_lower():
        for k in steps:
            @pl.when(jnp.logical_not(higher(k)))
            def _(k=k):
                column_copy(k).start()

    def answer_higher(late):
        for k in steps:
            crosses = (rank < 8) & (rank + k >= 8)
            @pl.when(higher(k) & (crosses if late else jnp.logical_not(crosses)))
            def _(k=k):
                column_arrived(k)
                column_copy(k).start()

    def hear_lower():
        for k in steps:
            @pl.when(jnp.logical_not(higher(k)))
            def _(k=k):
                column_arrived(k)

    def send_bulk():
        for copy in copy_plane:
            copy.start()
        for c in range(BLOCKS):
            for part in range(PER_BLOCK):
                x_copy(c * PER_BLOCK + part).start()
            y_copy(c).start()
        copy_core.start()

    def relay(r):
        x_copy(r).wait_recv()
        relay_copy(r).start()

    even, odd = lane_halves(BLK)
    ones = jnp.concatenate([even, odd], axis=0)

    def widen(v2):
        return jnp.concatenate([v2, ones], axis=1)

    def project(rows, place_k, place_v, blocks):
        for offset, place in ((0, place_k), (WIDTH, place_v)):
            for jj in range(0, PAIR, 2):
                part = dot(rows, wkv[:, offset + jj * BLK:offset + (jj + 2) * BLK])
                for j in range(jj, jj + 2):
                    for b in range(blocks):
                        piece = part[b * BLK:(b + 1) * BLK, (j - jj) * BLK:(j - jj + 1) * BLK].astype(BF)
                        ref = place(b, j)
                        ref[0:BLK] = piece * even
                        ref[BLK:2 * BLK] = piece * odd

    def own_queries():
        get_query.wait()
        for jj in range(0, PAIR, 2):
            part = dot(normed[...], wq[:, jj * BLK:(jj + 2) * BLK]) * SCORE_SCALE
            for j in range(jj, jj + 2):
                for b in range(BLOCKS):
                    qs[j, b] = part[b * BLK:(b + 1) * BLK, (j - jj) * BLK:(j - jj + 1) * BLK].astype(BF)

    def own_keys_values():
        get_key.wait()
        get_value.wait()
        project(normed[...], lambda b, j: own_k.at[j, b], lambda b, j: own_v.at[j, b], BLOCKS)

    def spread_masks():
        get_masks.wait()
        get_pairs.wait()
        get_partners.wait()
        live = counts[0]
        for qb in range(BLOCKS):
            for kb in range(BLOCKS):
                slot = jnp.int32(0)
                for s in range(SLOTS):
                    slot = jnp.where((pairs[0, s] == qb) & (pairs[1, s] == kb), s, slot)
                alive = jnp.where(slot < live, 1, 0)
                keep[qb, kb] = (mask_raw[slot] * alive).astype(F32).astype(BF)

    def attend_local(pair_range):
        for j in pair_range:
            q = qs[j].reshape(ROWS, BLK)
            for kb in range(BLOCKS):
                s = scores(q, own_k[j, kb])
                for b in range(BLOCKS):
                    mask = keep[b, kb]
                    p = jnp.exp2(s[b * BLK:(b + 1) * BLK]).astype(BF)
                    weights[j, b * BLK:(b + 1) * BLK, kb * 2 * BLK:(kb + 1) * 2 * BLK] = p * jnp.concatenate(
                        [mask, mask], axis=1
                    )
        for j in pair_range:
            v = jnp.concatenate([widen(own_v[j, kb]) for kb in range(BLOCKS)], axis=0)
            near[j] = dot(weights[j], v).reshape(BLOCKS, BLK, 2 * BLK)

    def project_core():
        project(land_core[...], lambda b, j: core_k.at[b, j], lambda b, j: core_v.at[b, j], BLOCKS)

    def attend_core():
        block = [partners[0, b] for b in range(BLOCKS)]
        for j in range(PAIR):
            for b in range(BLOCKS):
                weights[j, b * BLK:(b + 1) * BLK, 0:2 * BLK] = jnp.exp2(
                    scores(qs[j, b], core_k[block[b], j])
                ).astype(BF)
        for j in range(PAIR):
            for b in range(BLOCKS):
                near[j, b] += dot(weights[j, b * BLK:(b + 1) * BLK, 0:2 * BLK], widen(core_v[block[b], j]))

    def far_step(c, sources):
        lo, hi = sources[0], sources[-1] + 1
        rows = land[c, lo:hi].reshape((hi - lo) * BLK, WIDTH)
        project(rows, lambda b, j: far_k.at[lo + b, j], lambda b, j: far_v.at[lo + b, j], hi - lo)
        for m in sources:
            block = c - 1 if m == 2 else c
            target = jnp.int32(0)
            for b in range(BLOCKS):
                target = jnp.where(partners[m + 1, b] == block, b, target)
            for j in range(PAIR):
                far_w[m, j] = jnp.exp2(scores(qs[j, target], far_k[m, j])).astype(BF)
        for m in sources:
            block = c - 1 if m == 2 else c
            for j in range(PAIR):
                far_acc[m, block, j] = dot(far_w[m, j], widen(far_v[m, j]))

    def arrive_relayed(c):
        for part in range(PER_BLOCK):
            relay_copy(c * PER_BLOCK + part).wait_recv()

    def virtual_nodes():
        even_v, odd_v = lane_halves(VIRTUAL)
        ones_v = jnp.concatenate([even_v, odd_v], axis=0)
        table = gather.reshape(256, BLK)
        state = jnp.concatenate([table[pl.ds(i, VIRTUAL, stride=4), :] for i in range(4)], axis=1)
        virtual_kv = dot(norm_rows(state, gain), wkv[...]).astype(BF)
        for j in range(PAIR):
            for offset, ref in ((0, virt_k), (WIDTH, virt_v)):
                piece = virtual_kv[:, offset + j * BLK:offset + (j + 1) * BLK]
                ref[j, 0:VIRTUAL] = piece * even_v
                ref[j, VIRTUAL:2 * VIRTUAL] = piece * odd_v
        for j in range(PAIR):
            s = scores(qs[j].reshape(ROWS, BLK), virt_k[j])
            weights[j, :, 0:BLK] = jnp.exp2(s).astype(BF)
        for j in range(PAIR):
            wide = jnp.concatenate([virt_v[j], ones_v], axis=1)
            near[j] += dot(weights[j, :, 0:BLK], wide).reshape(BLOCKS, BLK, 2 * BLK)

    def add_far():
        for j in range(PAIR):
            for b in range(BLOCKS):
                near[j, b] += far_acc[0, partners[1, b], j] + far_acc[1, partners[2, b], j]

    def finish():
        for b in range(BLOCKS):
            for j in range(PAIR):
                total = near[j, b] + far_acc[2, partners[3, b], j]
                out_ref[b * BLK:(b + 1) * BLK, j * BLK:(j + 1) * BLK] = (
                    total[:, 0:BLK] / total[:, BLK:2 * BLK]
                ).astype(BF)

    pl.semaphore_wait(barrier, 15 + rank)
    send_bulk()
    own_queries()
    own_keys_values()
    spread_masks()
    attend_local((0, 1))
    for copy in copy_plane:
        copy.wait_recv()
    send_lower()
    relay(0)
    attend_local((2, 3))
    relay(1)
    copy_core.wait_recv()
    project_core()
    relay(2)
    attend_core()
    y_copy(0).wait_recv()
    far_step(0, (0, 1))
    relay(3)
    answer_higher(False)

    @pl.loop(1, BLOCKS)
    def _(c):
        y_copy(c).wait_recv()
        arrive_relayed(c - 1)
        far_step(c, (0, 1, 2))

        @pl.when(c < BLOCKS - 1)
        def _():
            for part in range(PER_BLOCK):
                relay((c + 1) * PER_BLOCK + part)

    for copy in copy_plane + [copy_core]:
        copy.wait_send()
    for r in range(RELAYS):
        x_copy(r).wait_send()
    for c in range(BLOCKS):
        y_copy(c).wait_send()
    answer_higher(True)
    hear_lower()
    virtual_nodes()
    add_far()
    for r in range(RELAYS - PER_BLOCK):
        relay_copy(r).wait_send()
    for k in steps:
        column_copy(k).wait_send()
    arrive_relayed(BLOCKS - 1)
    far_step(BLOCKS, (2,))
    finish()
    for r in range(RELAYS - PER_BLOCK, RELAYS):
        relay_copy(r).wait_send()


def local(
    features, norm_gain, w_query, key_weight, value_weight, w_out, virtual_states, block_pairs, block_masks,
    pair_counts, partners,
):
    dma = pltpu.SemaphoreType.DMA
    hbm = pl.BlockSpec(memory_space=pltpu.HBM)
    mixed = pl.pallas_call(
        kernel,
        out_shape=jax.ShapeDtypeStruct((ROWS, WIDTH), BF),
        in_specs=[hbm] * 8 + [pl.BlockSpec(memory_space=pltpu.SMEM), hbm],
        out_specs=pl.BlockSpec(memory_space=pltpu.VMEM),
        scratch_shapes=[
            pltpu.VMEM((1, WIDTH), F32),
            pltpu.VMEM((1, BLK), BF),
            pltpu.SMEM((2, SLOTS), jnp.int32),
            pltpu.SMEM((4, BLOCKS), jnp.int32),
            pltpu.VMEM((ROWS, WIDTH), BF),
            pltpu.VMEM((ROWS, WIDTH), BF),
            pltpu.VMEM((WIDTH, WIDTH), BF),
            pltpu.VMEM((WIDTH, 2 * WIDTH), BF),
            pltpu.VMEM((SLOTS, BLK, BLK), jnp.int32),
            pltpu.VMEM((BLOCKS, BLOCKS, BLK, BLK), BF),
            pltpu.VMEM((PAIR, BLOCKS, BLK, BLK), BF),
            pltpu.VMEM((PAIR, BLOCKS, 2 * BLK, BLK), BF),
            pltpu.VMEM((PAIR, BLOCKS, 2 * BLK, BLK), BF),
            pltpu.VMEM((ROWS, WIDTH), BF),
            pltpu.VMEM((BLOCKS, PAIR, 2 * BLK, BLK), BF),
            pltpu.VMEM((BLOCKS, PAIR, 2 * BLK, BLK), BF),
            pltpu.VMEM((BLOCKS + 1, 3, BLK, WIDTH), BF),
            pltpu.VMEM((3, PAIR, 2 * BLK, BLK), BF),
            pltpu.VMEM((3, PAIR, 2 * BLK, BLK), BF),
            pltpu.VMEM((PAIR, BLK, BLK), BF),
            pltpu.VMEM((PAIR, BLK, BLK), BF),
            pltpu.VMEM((16, 16, BLK), F32),
            pltpu.VMEM((PAIR, BLOCKS, BLK, 2 * BLK), F32),
            pltpu.VMEM((3, BLOCKS, PAIR, BLK, 2 * BLK), F32),
            pltpu.VMEM((PAIR, ROWS, 8 * BLK), BF),
            pltpu.VMEM((3, PAIR, BLK, 2 * BLK), BF),
            dma((9,)),
            dma((30,)), dma((30,)),
            dma((1,)), dma((1,)),
            dma((BLOCKS,)), dma((BLOCKS,)),
            dma((RELAYS,)), dma((RELAYS,)),
            dma((RELAYS,)), dma((RELAYS,)),
        ],
        compiler_params=pltpu.CompilerParams(
            collective_id=0, has_side_effects=True, vmem_limit_bytes=54500 * 1024
        ),
        cost_estimate=pl.CostEstimate(flops=8_000_000_000, bytes_accessed=4_500_000, transcendentals=4_500_000),
        name="expander_layer",
    )(
        features, norm_gain.reshape(1, WIDTH), w_query, key_weight, value_weight, virtual_states,
        block_pairs.T, block_masks, pair_counts, partners.reshape(4, BLOCKS),
    )
    return jnp.dot(mixed, w_out, preferred_element_type=F32).astype(BF)


def solution(mesh):
    placed = (
        P("nodes", None), P(), P(), P(), P(), P(), P("nodes", None), P("nodes", None), P("nodes", None, None),
        P("nodes"), P("nodes", None, None),
    )
    return jax.shard_map(local, mesh=mesh, in_specs=placed, out_specs=P("nodes", None), check_vma=False)
```

time: 45.8 us -> 31.7 us (0.69)
  the two profiles are of different devices: /device:TPU:1 before, /device:TPU:192 now
where the time goes in v2:
time: 31.7 us; the launch traced here: 31.5 us
  Pallas kernels  28.8 us (91%)
  matrix products  1.24 us (4%)
  between operations  0.76 us (2%)
  local copies, waits for them, and re-layouts  0.69 us (2%)
    pallas_call x1, Pallas kernels, local(): pl.pallas_call(kernel, out_shape=jax.ShapeDtypeStruct((ROWS, WIDTH), BF),...  28.8 us
    dot_general x1, matrix products, local(): return jnp.dot(mixed, w_out, preferred_element_type=F32).astype(BF)  1.24 us
    unnamed x10, local copies, waits for them, and re-layouts  0.69 us

profile of v2, /device:TPU:192, one launch (start us, length us, event | category | flops | bytes accessed | tf_op | source)
XLA Modules:
  0.0 31.5 jit_solution(11076934277814213343)
XLA Ops:
  0.0 0.0 copy-start
  0.7 0.0 copy-start.2
  0.7 0.0 copy-start.1
  0.7 0.0 copy-start.3
  0.7 0.0 copy-start.4
  0.8 0.6 %copy-done.2 = s32[1,4,4]{2,1,0:T(4,128)S(1)} copy-done((s32[1,4,4]{2,1,0:T(4,128)S(1)}, s32[1,4,4]{2,1,0:T(4,128)}, u32[]{:S(2)}) %copy-start.2) | copy-done | bytes 88
  1.4 0.0 copy-done.1
  1.4 0.0 copy-done.3
  1.4 0.0 copy-done.4
  1.4 28.8 %expander_layer.1 = bf16[512,512]{1,0:T(8,128)(2,1)S(1)} custom-call(bf16[512,512]{1,0:T(8,128)(2,1)} %features.1, f32[1,512]{1,0:T(1,128)S(1)} %bitcast.5, bf16[512,512]{1,0:T(8,128)(2,1)} %w_query.1, bf16[512,512]{1,0:T(8,128)(2,1)} %key_weight.1, bf16[512,512]{1,0:T(8,128)(2,1)} %value_weight.1, bf16[1,128]{1,0:T(2,128)(2,1)S(1)} %copy-done.4, ...), custom_call_target="tpu_custom_call" | custom-call | flops 8000000000 | bytes 4500000 | tf_op jit(solution)/shard_map/expander_layer/pallas_call | solution.py:375
  30.3 0.0 copy-done
  30.3 1.2 %convolution_convert_fusion = bf16[512,512]{1,0:T(8,128)(2,1)} fusion(bf16[512,512]{1,0:T(8,128)(2,1)S(1)} %expander_layer.1, bf16[512,512]{1,0:T(8,128)(2,1)S(1)} %copy-done), kind=kOutput, calls=%fused_computation | convolution fusion | flops 268697600 | bytes 1572864 | tf_op jit(solution)/shard_map/dot_general | solution.py:423
Async XLA Ops:
  0.0 30.3 %copy-start = (bf16[512,512]{1,0:T(8,128)(2,1)S(1)}, bf16[512,512]{1,0:T(8,128)(2,1)}, u32[]{:S(2)}) copy-start(bf16[512,512]{1,0:T(8,128)(2,1)} %param.16) | copy-start | bytes 1572868
  0.7 0.7 %copy-start.2 = (s32[1,4,4]{2,1,0:T(4,128)S(1)}, s32[1,4,4]{2,1,0:T(4,128)}, u32[]{:S(2)}) copy-start(s32[1,4,4]{2,1,0:T(4,128)} %param.21) | copy-start | bytes 196
  0.7 0.7 %copy-start.1 = (f32[512]{0:T(512)S(1)}, f32[512]{0:T(512)}, u32[]{:S(2)}) copy-start(f32[512]{0:T(512)} %param.12) | copy-start | bytes 6148
  0.7 0.7 %copy-start.3 = (s32[16,2]{0,1:T(2,128)S(1)}, s32[16,2]{0,1:T(2,128)}, u32[]{:S(2)}) copy-start(s32[16,2]{0,1:T(2,128)} %param.18) | copy-start | bytes 388
  0.7 0.7 %copy-start.4 = (bf16[1,128]{1,0:T(2,128)(2,1)S(1)}, bf16[1,128]{1,0:T(2,128)(2,1)}, u32[]{:S(2)}) copy-start(bf16[1,128]{1,0:T(2,128)(2,1)} %virtual_states.1) | copy-start | bytes 772

commit v3 on v2

--- a/solution.py
+++ b/solution.py
@@ -15,7 +15,7 @@
 PAIR = 4
 EPSILON = 1e-05
 SCORE_SCALE = 1.4426950408889634 / 8.0
-RELAY = 64
+RELAY = 32
 RELAYS = ROWS // RELAY
 PER_BLOCK = BLK // RELAY
 MESH = pl.DeviceIdType.MESH
@@ -49,7 +49,7 @@
     out_ref,
     gain_ref, virtual_row, pairs, partners, raw, normed, wq, wkv, mask_raw, keep, qs, own_k, own_v, land_core, core_k,
     core_v, land, far_k, far_v, virt_k, virt_v, gather, near, far_acc, weights, far_w,
-    local_sem, send_row, recv_row, send_core, recv_core, send_y, recv_y, send_x, recv_x, send_relay, recv_relay,
+    local_sem, send_row, recv_row, send_core, recv_core, send_y, recv_y, send_x, recv_x, send_relay, recv_relay, entered, token,
 ):
     me = lax.axis_index("nodes")
     core = me % 2
@@ -67,18 +67,19 @@
     x_peer = device(x_near, z, y, core)
     relay_peer = device(3 - x, z, y, core)
     plane = []
-    for dx in range(4):
+    for flip_x in range(2):
         for flip_y in range(2):
             for flip_core in range(2):
-                if dx or flip_y or flip_core:
+                if flip_x or flip_y or flip_core:
                     plane.append(
-                        device((x + dx) % 4, z, y_near if flip_y else y, 1 - core if flip_core else core)
+                        device(x_near if flip_x else x, z, y_near if flip_y else y, 1 - core if flip_core else core)
                     )
+
     half = y // 2
-    rank = jnp.where(z < 4, z * 2 + half, 8 + half * 4 + z - 4)
+    rank = jnp.where(z < 4, z * 2 + half, 8 + half * 4 + 7 - z)
 
     def ranked(r):
-        zz = jnp.where(r < 8, r // 2, 4 + r % 4)
+        zz = jnp.where(r < 8, r // 2, 7 - r % 4)
         hh = jnp.where(r < 8, r % 2, (r - 8) // 4)
         return device(x, zz, jnp.where(hh == half, y, 3 - y), core)
 
@@ -88,13 +89,10 @@
     def higher(k):
         return rank + k < 16
 
-    barrier = pltpu.get_barrier_semaphore()
-    for peer in plane:
-        pl.semaphore_signal(barrier, inc=1, device_id=(peer,), device_id_type=MESH)
-    for k in steps:
-        @pl.when(higher(k))
-        def _(k=k):
-            pl.semaphore_signal(barrier, inc=1, device_id=(columns[k],), device_id_type=MESH)
+    remote_eight = (rank >= 8) & (rank < 11)
+
+    def hears_later(k):
+        return (rank == 7) & (k < 4)
 
     def fetch(src, dst, index):
         copy = pltpu.make_async_copy(src, dst, local_sem.at[index])
@@ -102,14 +100,28 @@
         return copy
 
     get_features = fetch(features, raw, 0)
+    get_row = fetch(virtual_states, virtual_row, 2)
+    barrier = pltpu.get_barrier_semaphore()
+    for k in steps:
+        @pl.when(higher(k) & jnp.logical_not(hears_later(k)))
+        def _(k=k):
+            pl.semaphore_signal(barrier, inc=1, device_id=(columns[k],), device_id_type=MESH)
+    for peer in plane:
+        pl.semaphore_signal(barrier, inc=1, device_id=(peer,), device_id_type=MESH)
+    @pl.when(x < 2)
+    def _():
+        pl.semaphore_signal(barrier, inc=1, device_id=(relay_peer,), device_id_type=MESH)
+
     get_gain = fetch(norm_gain, gain_ref, 1)
-    get_row = fetch(virtual_states, virtual_row, 2)
     get_query = fetch(w_query, wq, 3)
     get_key = fetch(key_weight, wkv.at[:, pl.ds(0, WIDTH)], 4)
     get_value = fetch(value_weight, wkv.at[:, pl.ds(WIDTH, WIDTH)], 5)
     get_pairs = fetch(block_pairs, pairs, 6)
     get_partners = fetch(partner_blocks, partners, 7)
     get_masks = fetch(masks, mask_raw, 8)
+
+    def partner(m, b):
+        return partners[m, b]
 
     group = z * 2 + y // 2
     member = x * 4 + (y % 2) * 2 + core
@@ -149,13 +161,36 @@
     copy_core = remote(normed, land_core, send_core.at[0], recv_core.at[0], core_peer)
     mine = gather.at[group, pl.ds(member, 1)]
     copy_plane = [remote(mine, mine, send_row.at[i], recv_row.at[i], peer) for i, peer in enumerate(plane)]
+    eight = gather.at[group, pl.ds(pl.multiple_of(8 * (x // 2), 8), 8)]
+    copy_across = remote(eight, eight, send_row.at[7], recv_row.at[7], relay_peer)
     sixteen = gather.at[group]
 
     def column_copy(k):
-        return remote(sixteen, sixteen, send_row.at[14 + k], recv_row.at[14 + k], columns[k])
+        return remote(sixteen, sixteen, send_row.at[7 + k], recv_row.at[7 + k], columns[k])
 
     def column_arrived(k):
         column_copy(16 - k).wait_recv()
+
+    def tell_lower():
+        @pl.when(x >= 2)
+        def _():
+            pl.semaphore_signal(entered.at[2], inc=1, device_id=(relay_peer,), device_id_type=MESH)
+        @pl.when(rank == 11)
+        def _():
+            for k in (13, 14, 15):
+                pl.semaphore_signal(token, inc=1, device_id=(columns[k],), device_id_type=MESH)
+        for k in steps:
+            @pl.when(jnp.logical_not(higher(k)) & jnp.logical_not(remote_eight & (rank + k == 16 + 7)))
+            def _(k=k):
+                crosses = jnp.where((rank >= 8) & (rank + k - 16 < 8), 1, 0)
+                pl.semaphore_signal(entered.at[crosses], inc=1, device_id=(columns[k],), device_id_type=MESH)
+
+    def tell_rank_seven():
+        @pl.when(remote_eight)
+        def _():
+            pl.semaphore_wait(token, 1)
+            seven = ranked(7)
+            pl.semaphore_signal(entered.at[1], inc=1, device_id=(seven,), device_id_type=MESH)
 
     def send_lower():
         for k in steps:
@@ -163,19 +198,21 @@
             def _(k=k):
                 column_copy(k).start()
 
-    def answer_higher(late):
+    def send_higher_near():
+        @pl.when(rank % 8 < 7)
+        def _():
+            pl.semaphore_wait(entered.at[0], 7 - rank % 8)
+        for k in range(1, 8):
+            @pl.when(rank % 8 + k < 8)
+            def _(k=k):
+                column_copy(k).start()
+
+    def send_higher_far():
+        pl.semaphore_wait(entered.at[1], 8)
         for k in steps:
-            crosses = (rank < 8) & (rank + k >= 8)
-            @pl.when(higher(k) & (crosses if late else jnp.logical_not(crosses)))
+            @pl.when((rank + k >= 8) & higher(k))
             def _(k=k):
-                column_arrived(k)
                 column_copy(k).start()
-
-    def hear_lower():
-        for k in steps:
-            @pl.when(jnp.logical_not(higher(k)))
-            def _(k=k):
-                column_arrived(k)
 
     def send_bulk():
         for copy in copy_plane:
@@ -186,9 +223,11 @@
             y_copy(c).start()
         copy_core.start()
 
-    def relay(r):
-        x_copy(r).wait_recv()
-        relay_copy(r).start()
+    def relay(half_block):
+        for part in range(BLK // 2 // RELAY):
+            r = half_block * (BLK // 2 // RELAY) + part
+            x_copy(r).wait_recv()
+            relay_copy(r).start()
 
     even, odd = lane_halves(BLK)
     ones = jnp.concatenate([even, odd], axis=0)
@@ -252,7 +291,7 @@
         project(land_core[...], lambda b, j: core_k.at[b, j], lambda b, j: core_v.at[b, j], BLOCKS)
 
     def attend_core():
-        block = [partners[0, b] for b in range(BLOCKS)]
+        block = [partner(0, b) for b in range(BLOCKS)]
         for j in range(PAIR):
             for b in range(BLOCKS):
                 weights[j, b * BLK:(b + 1) * BLK, 0:2 * BLK] = jnp.exp2(
@@ -270,7 +309,7 @@
             block = c - 1 if m == 2 else c
             target = jnp.int32(0)
             for b in range(BLOCKS):
-                target = jnp.where(partners[m + 1, b] == block, b, target)
+                target = jnp.where(partner(m + 1, b) == block, b, target)
             for j in range(PAIR):
                 far_w[m, j] = jnp.exp2(scores(qs[j, target], far_k[m, j])).astype(BF)
         for m in sources:
@@ -303,57 +342,75 @@
     def add_far():
         for j in range(PAIR):
             for b in range(BLOCKS):
-                near[j, b] += far_acc[0, partners[1, b], j] + far_acc[1, partners[2, b], j]
+                near[j, b] += far_acc[0, partner(1, b), j] + far_acc[1, partner(2, b), j]
 
     def finish():
         for b in range(BLOCKS):
             for j in range(PAIR):
-                total = near[j, b] + far_acc[2, partners[3, b], j]
+                total = near[j, b] + far_acc[2, partner(3, b), j]
                 out_ref[b * BLK:(b + 1) * BLK, j * BLK:(j + 1) * BLK] = (
                     total[:, 0:BLK] / total[:, BLK:2 * BLK]
                 ).astype(BF)
 
-    pl.semaphore_wait(barrier, 15 + rank)
+    pl.semaphore_wait(barrier, 7 + x // 2 + rank - jnp.where(remote_eight, 1, 0))
     send_bulk()
+    tell_lower()
     own_queries()
     own_keys_values()
+    tell_rank_seven()
     spread_masks()
     attend_local((0, 1))
     for copy in copy_plane:
         copy.wait_recv()
-    send_lower()
+
+    @pl.when(x < 2)
+    def _():
+        pl.semaphore_wait(entered.at[2], 1)
+    copy_across.start()
     relay(0)
     attend_local((2, 3))
     relay(1)
     copy_core.wait_recv()
     project_core()
+    copy_across.wait_recv()
+    send_lower()
     relay(2)
     attend_core()
+    send_higher_near()
     y_copy(0).wait_recv()
     far_step(0, (0, 1))
     relay(3)
-    answer_higher(False)
 
     @pl.loop(1, BLOCKS)
     def _(c):
+        @pl.when((z < 4) & (c == 2 - z // 2))
+        def _():
+            send_higher_far()
+
         y_copy(c).wait_recv()
         arrive_relayed(c - 1)
         far_step(c, (0, 1, 2))
 
         @pl.when(c < BLOCKS - 1)
         def _():
-            for part in range(PER_BLOCK):
-                relay((c + 1) * PER_BLOCK + part)
-
-    for copy in copy_plane + [copy_core]:
+            relay(2 * c + 2)
+
+        @pl.when(c == 3)
+        def _():
+            for k in steps:
+                column_arrived(k)
+            virtual_nodes()
+
+        @pl.when(c < BLOCKS - 1)
+        def _():
+            relay(2 * c + 3)
+
+    for copy in copy_plane + [copy_across, copy_core]:
         copy.wait_send()
     for r in range(RELAYS):
         x_copy(r).wait_send()
     for c in range(BLOCKS):
         y_copy(c).wait_send()
-    answer_higher(True)
-    hear_lower()
-    virtual_nodes()
     add_far()
     for r in range(RELAYS - PER_BLOCK):
         relay_copy(r).wait_send()
@@ -405,11 +462,13 @@
             pltpu.VMEM((PAIR, ROWS, 8 * BLK), BF),
             pltpu.VMEM((3, PAIR, BLK, 2 * BLK), BF),
             dma((9,)),
-            dma((30,)), dma((30,)),
+            dma((23,)), dma((23,)),
             dma((1,)), dma((1,)),
             dma((BLOCKS,)), dma((BLOCKS,)),
             dma((RELAYS,)), dma((RELAYS,)),
             dma((RELAYS,)), dma((RELAYS,)),
+            pltpu.SemaphoreType.REGULAR((3,)),
+            pltpu.SemaphoreType.REGULAR,
         ],
         compiler_params=pltpu.CompilerParams(
             collective_id=0, has_side_effects=True, vmem_limit_bytes=54500 * 1024

time: 31.7 us -> 27.1 us (0.85)
  Pallas kernels: 28.8 us -> 24.3 us
    pallas_call x1, Pallas kernels: 28.8 us -> 24.3 us  [local(): pl.pallas_call(kernel, out_shape=jax.ShapeDtypeStruct((ROWS, WIDTH), BF),...]
where the time goes in v3:
time: 27.1 us; the launch traced here: 26.9 us
  Pallas kernels  24.3 us (90%)
  matrix products  1.24 us (5%)
  between operations  0.76 us (3%)
  local copies, waits for them, and re-layouts  0.69 us (3%)
    pallas_call x1, Pallas kernels, local(): pl.pallas_call(kernel, out_shape=jax.ShapeDtypeStruct((ROWS, WIDTH), BF),...  24.3 us
    dot_general x1, matrix products, local(): return jnp.dot(mixed, w_out, preferred_element_type=F32).astype(BF)  1.24 us
    unnamed x10, local copies, waits for them, and re-layouts  0.69 us

profile of v3, /device:TPU:192, one launch (start us, length us, event | category | flops | bytes accessed | tf_op | source)
XLA Modules:
  0.0 26.9 jit_solution(6640711781185710583)
XLA Ops:
  0.0 0.0 copy-start
  0.7 0.0 copy-start.2
  0.7 0.0 copy-start.1
  0.7 0.0 copy-start.3
  0.7 0.0 copy-start.4
  0.8 0.6 %copy-done.2 = s32[1,4,4]{2,1,0:T(4,128)S(1)} copy-done((s32[1,4,4]{2,1,0:T(4,128)S(1)}, s32[1,4,4]{2,1,0:T(4,128)}, u32[]{:S(2)}) %copy-start.2) | copy-done | bytes 88
  1.4 0.0 copy-done.1
  1.4 0.0 copy-done.3
  1.4 0.0 copy-done.4
  1.4 24.3 %expander_layer.1 = bf16[512,512]{1,0:T(8,128)(2,1)S(1)} custom-call(bf16[512,512]{1,0:T(8,128)(2,1)} %features.1, f32[1,512]{1,0:T(1,128)S(1)} %bitcast.5, bf16[512,512]{1,0:T(8,128)(2,1)} %w_query.1, bf16[512,512]{1,0:T(8,128)(2,1)} %key_weight.1, bf16[512,512]{1,0:T(8,128)(2,1)} %value_weight.1, bf16[1,128]{1,0:T(2,128)(2,1)S(1)} %copy-done.4, ...), custom_call_target="tpu_custom_call" | custom-call | flops 8000000000 | bytes 4500000 | tf_op jit(solution)/shard_map/expander_layer/pallas_call | solution.py:432
  25.7 0.0 copy-done
  25.7 1.2 %convolution_convert_fusion = bf16[512,512]{1,0:T(8,128)(2,1)} fusion(bf16[512,512]{1,0:T(8,128)(2,1)S(1)} %expander_layer.1, bf16[512,512]{1,0:T(8,128)(2,1)S(1)} %copy-done), kind=kOutput, calls=%fused_computation | convolution fusion | flops 268697600 | bytes 1572864 | tf_op jit(solution)/shard_map/dot_general | solution.py:482
Async XLA Ops:
  0.0 25.7 %copy-start = (bf16[512,512]{1,0:T(8,128)(2,1)S(1)}, bf16[512,512]{1,0:T(8,128)(2,1)}, u32[]{:S(2)}) copy-start(bf16[512,512]{1,0:T(8,128)(2,1)} %param.16) | copy-start | bytes 1572868
  0.7 0.7 %copy-start.2 = (s32[1,4,4]{2,1,0:T(4,128)S(1)}, s32[1,4,4]{2,1,0:T(4,128)}, u32[]{:S(2)}) copy-start(s32[1,4,4]{2,1,0:T(4,128)} %param.21) | copy-start | bytes 196
  0.7 0.7 %copy-start.1 = (f32[512]{0:T(512)S(1)}, f32[512]{0:T(512)}, u32[]{:S(2)}) copy-start(f32[512]{0:T(512)} %param.12) | copy-start | bytes 6148
  0.7 0.7 %copy-start.3 = (s32[16,2]{0,1:T(2,128)S(1)}, s32[16,2]{0,1:T(2,128)}, u32[]{:S(2)}) copy-start(s32[16,2]{0,1:T(2,128)} %param.18) | copy-start | bytes 388
  0.7 0.7 %copy-start.4 = (bf16[1,128]{1,0:T(2,128)(2,1)S(1)}, bf16[1,128]{1,0:T(2,128)(2,1)}, u32[]{:S(2)}) copy-start(bf16[1,128]{1,0:T(2,128)(2,1)} %virtual_states.1) | copy-start | bytes 772

commit v4 on v3

--- a/solution.py
+++ b/solution.py
@@ -30,7 +30,7 @@
 
 
 def scores(q, k2):
-    return lax.dot_general(q, k2, (((1,), (1,)), ((), ())), preferred_element_type=F32)
+    return lax.dot_general(q, k2, (((1,), (1,)), ((), ())), preferred_element_type=F32) * SCORE_SCALE
 
 
 def dot(a, b):
@@ -102,27 +102,17 @@
     get_features = fetch(features, raw, 0)
     get_row = fetch(virtual_states, virtual_row, 2)
     barrier = pltpu.get_barrier_semaphore()
-    for k in steps:
-        @pl.when(higher(k) & jnp.logical_not(hears_later(k)))
-        def _(k=k):
-            pl.semaphore_signal(barrier, inc=1, device_id=(columns[k],), device_id_type=MESH)
     for peer in plane:
         pl.semaphore_signal(barrier, inc=1, device_id=(peer,), device_id_type=MESH)
     @pl.when(x < 2)
     def _():
         pl.semaphore_signal(barrier, inc=1, device_id=(relay_peer,), device_id_type=MESH)
+    for k in steps:
+        @pl.when(higher(k) & jnp.logical_not(hears_later(k)))
+        def _(k=k):
+            pl.semaphore_signal(barrier, inc=1, device_id=(columns[k],), device_id_type=MESH)
 
     get_gain = fetch(norm_gain, gain_ref, 1)
-    get_query = fetch(w_query, wq, 3)
-    get_key = fetch(key_weight, wkv.at[:, pl.ds(0, WIDTH)], 4)
-    get_value = fetch(value_weight, wkv.at[:, pl.ds(WIDTH, WIDTH)], 5)
-    get_pairs = fetch(block_pairs, pairs, 6)
-    get_partners = fetch(partner_blocks, partners, 7)
-    get_masks = fetch(masks, mask_raw, 8)
-
-    def partner(m, b):
-        return partners[m, b]
-
     group = z * 2 + y // 2
     member = x * 4 + (y % 2) * 2 + core
     get_row.wait()
@@ -130,6 +120,15 @@
     get_gain.wait()
     gain = gain_ref[...]
     get_features.wait()
+    get_query = fetch(w_query, wq, 3)
+    get_key = fetch(key_weight, wkv.at[:, pl.ds(0, WIDTH)], 4)
+    get_value = fetch(value_weight, wkv.at[:, pl.ds(WIDTH, WIDTH)], 5)
+    get_pairs = fetch(block_pairs, pairs, 6)
+    get_partners = fetch(partner_blocks, partners, 7)
+    get_masks = fetch(masks, mask_raw, 8)
+
+    def partner(m, b):
+        return partners[m, b]
     for block in range(BLOCKS):
         rows = pl.ds(block * BLK, BLK)
         normed[rows] = norm_rows(raw[rows].astype(F32), gain)
@@ -215,11 +214,13 @@
                 column_copy(k).start()
 
     def send_bulk():
+        x_copy(0).start()
         for copy in copy_plane:
             copy.start()
         for c in range(BLOCKS):
             for part in range(PER_BLOCK):
-                x_copy(c * PER_BLOCK + part).start()
+                if c or part:
+                    x_copy(c * PER_BLOCK + part).start()
             y_copy(c).start()
         copy_core.start()
 
@@ -249,7 +250,7 @@
     def own_queries():
         get_query.wait()
         for jj in range(0, PAIR, 2):
-            part = dot(normed[...], wq[:, jj * BLK:(jj + 2) * BLK]) * SCORE_SCALE
+            part = dot(normed[...], wq[:, jj * BLK:(jj + 2) * BLK])
             for j in range(jj, jj + 2):
                 for b in range(BLOCKS):
                     qs[j, b] = part[b * BLK:(b + 1) * BLK, (j - jj) * BLK:(j - jj + 1) * BLK].astype(BF)
@@ -421,6 +422,17 @@
     finish()
     for r in range(RELAYS - PER_BLOCK, RELAYS):
         relay_copy(r).wait_send()
+
+
+def out_kernel(mixed, w_ref, out_ref, rows, sems):
+    copies = []
+    for b in range(BLOCKS):
+        part = pl.ds(b * BLK, BLK)
+        rows[part] = dot(mixed[part], w_ref[...]).astype(BF)
+        copies.append(pltpu.make_async_copy(rows.at[part], out_ref.at[part], sems.at[b]))
+        copies[b].start()
+    for copy in copies:
+        copy.wait()
 
 
 def local(
@@ -476,10 +488,27 @@
         cost_estimate=pl.CostEstimate(flops=8_000_000_000, bytes_accessed=4_500_000, transcendentals=4_500_000),
         name="expander_layer",
     )(
-        features, norm_gain.reshape(1, WIDTH), w_query, key_weight, value_weight, virtual_states,
-        block_pairs.T, block_masks, pair_counts, partners.reshape(4, BLOCKS),
+        *(
+            pltpu.with_memory_space_constraint(a, pltpu.HBM)
+            for a in (
+                features, norm_gain.reshape(1, WIDTH), w_query, key_weight, value_weight, virtual_states,
+                block_pairs.T, block_masks,
+            )
+        ),
+        pair_counts,
+        pltpu.with_memory_space_constraint(partners.reshape(4, BLOCKS), pltpu.HBM),
     )
-    return jnp.dot(mixed, w_out, preferred_element_type=F32).astype(BF)
+    vmem = pl.BlockSpec(memory_space=pltpu.VMEM)
+    return pl.pallas_call(
+        out_kernel,
+        out_shape=jax.ShapeDtypeStruct((ROWS, WIDTH), BF),
+        in_specs=[vmem, vmem],
+        out_specs=hbm,
+        scratch_shapes=[pltpu.VMEM((ROWS, WIDTH), BF), dma((BLOCKS,))],
+        compiler_params=pltpu.CompilerParams(vmem_limit_bytes=8 * 1024 * 1024),
+        cost_estimate=pl.CostEstimate(flops=270_000_000, bytes_accessed=1_600_000, transcendentals=0),
+        name="out_projection",
+    )(mixed, w_out)
 
 
 def solution(mesh):

time: 27.1 us -> 26.4 us (0.974)
  matrix products: 1.24 us -> 0 us
  Pallas kernels: 24.3 us -> 25.5 us
  local copies, waits for them, and re-layouts: 0.69 us -> 0.01 us
    dot_general x1 -> x0, matrix products: 1.24 us -> none  [local(): return jnp.dot(mixed, w_out, preferred_element_type=F32).astype(BF)]
    pallas_call x0 -> x1, Pallas kernels: none -> 1.14 us  [local(): pl.pallas_call(out_kernel, out_shape=jax.ShapeDtypeStruct((ROWS, WIDTH),...]
    unnamed x10 -> x2, local copies, waits for them, and re-layouts: 0.69 us -> 0.01 us
where the time goes in v4:
time: 26.4 us; the launch traced here: 26.2 us
  Pallas kernels  25.5 us (97%)
  between operations  0.68 us (3%)
    pallas_call x1, Pallas kernels, local(): pl.pallas_call(kernel, out_shape=jax.ShapeDtypeStruct((ROWS, WIDTH), BF),...  24.4 us
    pallas_call x1, Pallas kernels, local(): pl.pallas_call(out_kernel, out_shape=jax.ShapeDtypeStruct((ROWS, WIDTH),...  1.14 us

profile of v4, /device:TPU:192, one launch (start us, length us, event | category | flops | bytes accessed | tf_op | source)
XLA Modules:
  0.0 26.2 jit_solution(13343217922649668007)
XLA Ops:
  0.7 0.0 copy-start
  0.7 24.4 %expander_layer.1.mixed = bf16[512,512]{1,0:T(8,128)(2,1)S(1)} custom-call(bf16[512,512]{1,0:T(8,128)(2,1)} %features.1, f32[1,512]{1,0:T(1,128)} %bitcast.3, bf16[512,512]{1,0:T(8,128)(2,1)} %w_query.1, bf16[512,512]{1,0:T(8,128)(2,1)} %key_weight.1, bf16[512,512]{1,0:T(8,128)(2,1)} %value_weight.1, bf16[1,128]{1,0:T(2,128)(2,1)} %virtual_states.1, ...), custom_call_target="tpu_custom_call" | custom-call | flops 8000000000 | bytes 4500000 | tf_op jit(solution)/shard_map/expander_layer/pallas_call | solution.py:444
  25.1 0.0 copy-done
  25.1 1.1 %out_projection.1 = bf16[512,512]{1,0:T(8,128)(2,1)} custom-call(bf16[512,512]{1,0:T(8,128)(2,1)S(1)} %expander_layer.1.mixed, bf16[512,512]{1,0:T(8,128)(2,1)S(1)} %copy-done), custom_call_target="tpu_custom_call" | custom-call | flops 270000000 | bytes 1600000 | tf_op jit(solution)/shard_map/out_projection/pallas_call | solution.py:502
Async XLA Ops:
  0.7 24.4 %copy-start = (bf16[512,512]{1,0:T(8,128)(2,1)S(1)}, bf16[512,512]{1,0:T(8,128)(2,1)}, u32[]{:S(2)}) copy-start(bf16[512,512]{1,0:T(8,128)(2,1)} %w_ref.1) | copy-start | bytes 1572868

commit v5 on v4

--- a/solution.py
+++ b/solution.py
@@ -389,12 +389,14 @@
             send_higher_far()
 
         y_copy(c).wait_recv()
+        far_step(c, (0, 1))
+
+        @pl.when(c < BLOCKS - 1)
+        def _():
+            relay(2 * c + 2)
+
         arrive_relayed(c - 1)
-        far_step(c, (0, 1, 2))
-
-        @pl.when(c < BLOCKS - 1)
-        def _():
-            relay(2 * c + 2)
+        far_step(c, (2,))
 
         @pl.when(c == 3)
         def _():

time: 26.4 us -> 26.2 us (level)
  no operation moved by 1% of the time
where the time goes in v5:
time: 26.2 us; the launch traced here: 26.1 us
  Pallas kernels  25.4 us (97%)
  between operations  0.68 us (3%)
    pallas_call x1, Pallas kernels, local(): pl.pallas_call(kernel, out_shape=jax.ShapeDtypeStruct((ROWS, WIDTH), BF),...  24.2 us
    pallas_call x1, Pallas kernels, local(): pl.pallas_call(out_kernel, out_shape=jax.ShapeDtypeStruct((ROWS, WIDTH),...  1.14 us

profile of v5, /device:TPU:192, one launch (start us, length us, event | category | flops | bytes accessed | tf_op | source)
XLA Modules:
  0.0 26.1 jit_solution(12175705909315904960)
XLA Ops:
  0.7 0.0 copy-start
  0.7 24.2 %expander_layer.1.mixed = bf16[512,512]{1,0:T(8,128)(2,1)S(1)} custom-call(bf16[512,512]{1,0:T(8,128)(2,1)} %features.1, f32[1,512]{1,0:T(1,128)} %bitcast.3, bf16[512,512]{1,0:T(8,128)(2,1)} %w_query.1, bf16[512,512]{1,0:T(8,128)(2,1)} %key_weight.1, bf16[512,512]{1,0:T(8,128)(2,1)} %value_weight.1, bf16[1,128]{1,0:T(2,128)(2,1)} %virtual_states.1, ...), custom_call_target="tpu_custom_call" | custom-call | flops 8000000000 | bytes 4500000 | tf_op jit(solution)/shard_map/expander_layer/pallas_call | solution.py:446
  24.9 0.0 copy-done
  24.9 1.1 %out_projection.1 = bf16[512,512]{1,0:T(8,128)(2,1)} custom-call(bf16[512,512]{1,0:T(8,128)(2,1)S(1)} %expander_layer.1.mixed, bf16[512,512]{1,0:T(8,128)(2,1)S(1)} %copy-done), custom_call_target="tpu_custom_call" | custom-call | flops 270000000 | bytes 1600000 | tf_op jit(solution)/shard_map/out_projection/pallas_call | solution.py:504
Async XLA Ops:
  0.7 24.3 %copy-start = (bf16[512,512]{1,0:T(8,128)(2,1)S(1)}, bf16[512,512]{1,0:T(8,128)(2,1)}, u32[]{:S(2)}) copy-start(bf16[512,512]{1,0:T(8,128)(2,1)} %w_ref.1) | copy-start | bytes 1572868

commit v6 on v5

--- a/solution.py
+++ b/solution.py
@@ -358,9 +358,9 @@
     tell_lower()
     own_queries()
     own_keys_values()
-    tell_rank_seven()
     spread_masks()
     attend_local((0, 1))
+    tell_rank_seven()
     for copy in copy_plane:
         copy.wait_recv()
 
@@ -377,10 +377,10 @@
     send_lower()
     relay(2)
     attend_core()
-    send_higher_near()
     y_copy(0).wait_recv()
     far_step(0, (0, 1))
     relay(3)
+    send_higher_near()
 
     @pl.loop(1, BLOCKS)
     def _(c):

time: 26.2 us -> 26.1 us (level)
  no operation moved by 1% of the time
where the time goes in v6:
time: 26.1 us; the launch traced here: 26 us
  Pallas kernels  25.3 us (97%)
  between operations  0.68 us (3%)
    pallas_call x1, Pallas kernels, local(): pl.pallas_call(kernel, out_shape=jax.ShapeDtypeStruct((ROWS, WIDTH), BF),...  24.2 us
    pallas_call x1, Pallas kernels, local(): pl.pallas_call(out_kernel, out_shape=jax.ShapeDtypeStruct((ROWS, WIDTH),...  1.13 us

profile of v6, /device:TPU:192, one launch (start us, length us, event | category | flops | bytes accessed | tf_op | source)
XLA Modules:
  0.0 26.0 jit_solution(3880998961331072752)
XLA Ops:
  0.7 0.0 copy-start
  0.7 24.2 %expander_layer.1.mixed = bf16[512,512]{1,0:T(8,128)(2,1)S(1)} custom-call(bf16[512,512]{1,0:T(8,128)(2,1)} %features.1, f32[1,512]{1,0:T(1,128)} %bitcast.3, bf16[512,512]{1,0:T(8,128)(2,1)} %w_query.1, bf16[512,512]{1,0:T(8,128)(2,1)} %key_weight.1, bf16[512,512]{1,0:T(8,128)(2,1)} %value_weight.1, bf16[1,128]{1,0:T(2,128)(2,1)} %virtual_states.1, ...), custom_call_target="tpu_custom_call" | custom-call | flops 8000000000 | bytes 4500000 | tf_op jit(solution)/shard_map/expander_layer/pallas_call | solution.py:446
  24.9 0.0 copy-done
  24.9 1.1 %out_projection.1 = bf16[512,512]{1,0:T(8,128)(2,1)} custom-call(bf16[512,512]{1,0:T(8,128)(2,1)S(1)} %expander_layer.1.mixed, bf16[512,512]{1,0:T(8,128)(2,1)S(1)} %copy-done), custom_call_target="tpu_custom_call" | custom-call | flops 270000000 | bytes 1600000 | tf_op jit(solution)/shard_map/out_projection/pallas_call | solution.py:504
Async XLA Ops:
  0.7 24.2 %copy-start = (bf16[512,512]{1,0:T(8,128)(2,1)S(1)}, bf16[512,512]{1,0:T(8,128)(2,1)}, u32[]{:S(2)}) copy-start(bf16[512,512]{1,0:T(8,128)(2,1)} %w_ref.1) | copy-start | bytes 1572868
